TPU v7x, 32 devices: a whole 2x2x4 slice. The times are simulated.
32 devices in a mesh: section: 4 (over y, x), dp: 8 (over z, core).
Axes of the slice: x: 2, y: 2, z: 4, core: 2. Of those that a mesh axis runs over, the one named last changes fastest.
Arguments:
- inputs: bfloat16 [4096, 768], P('dp'), may hold values from -6 to 6
- cotangent: bfloat16 [4096, 768], P('dp'), may hold values from -6 to 6
- long_count: int32 [8, 2], P('dp'), may hold values from 0 to 1, as said below
- timesteps: int32 [8, 2, 2], P('dp'), may hold values from 0 to 999
- w_qkv: bfloat16 [4, 768, 2304], P('section'), may hold values from -0.21875 to 0.21875
- w_out: bfloat16 [4, 768, 768], P('section'), may hold values from -0.625 to 0.625
- w_in: bfloat16 [4, 768, 3072], P('section'), may hold values from -0.21875 to 0.21875
- w_down: bfloat16 [4, 3072, 768], P('section'), may hold values from -0.109375 to 0.109375
- ada_weight: bfloat16 [4, 128, 4608], P('section'), may hold values from -0.5 to 0.5
Outputs:
- hidden_out: bfloat16 [4, 4096, 768], P('section', 'dp')
- grad_in: bfloat16 [4, 4096, 768], P('section', 'dp')
- grad_qkv: float32 [4, 768, 2304], P('section', 'dp')
- grad_out: float32 [4, 768, 768], P('section', 'dp')
- grad_up: float32 [4, 768, 3072], P('section', 'dp')
- grad_down: float32 [4, 3072, 768], P('section', 'dp')
- grad_ada: float32 [4, 128, 4608], P('section', 'dp')
Inputs may be any that keep to these rules, and one draw needn't show every extreme that they name: `long_count`: 1 where the micro-batch holds one sequence of 256 tokens, 0 where it holds 2 sequences of 128; both values occur in every draw.
All inputs are finite; a program needn't handle non-finite values.
Results may differ from a plain program's by a relative error of at most 0.015.
Values may be sent and summed in bfloat16 or wider, within the bound.
A program may use at most 576 MiB of HBM per device.

v0:
```python
import math

import jax
import jax.numpy as jnp
from jax import lax
from jax.sharding import PartitionSpec as P

HEADS = 12
TEMB = 128
SHORT = 128


norm_eps = 1e-06
highest = lax.Precision.HIGHEST


def shifted(block, axis, distance):
    devices = range(lax.axis_size(axis))
    route = [(i - distance, i) for i in devices if i - distance in devices]
    return lax.ppermute(block, axis, route)


def time_features(timestep_ids):
    half_width = TEMB // 2
    frequency = jnp.exp(-math.log(10000.0) * jnp.arange(half_width, dtype=jnp.float32) / half_width)
    angles = timestep_ids.astype(jnp.float32)[:, None] * 0.1 * frequency[None, :]
    return jnp.concatenate([jnp.sin(angles), jnp.cos(angles)], axis=1)


def modulate(hidden, shift_part, scale_part):
    centered = hidden - jnp.mean(hidden, axis=-1, keepdims=True)
    variance = jnp.mean(centered * centered, axis=-1, keepdims=True)
    return centered * lax.rsqrt(variance + norm_eps) * (1.0 + scale_part) + shift_part


def smooth_gate(pre_values):
    return jax.nn.gelu(pre_values, approximate=True)


def low_dot(left_side, right_side):
    return jnp.dot(left_side, right_side, preferred_element_type=jnp.float32)


def place_row(buffer, target, piece):
    return buffer.at[target].set(piece, mode="drop")


def split_heads(packed, part_index):
    row_count = packed.shape[0]
    feature_width = packed.shape[1] // 3
    piece = packed[:, part_index * feature_width : (part_index + 1) * feature_width]
    return piece.reshape(row_count, HEADS, feature_width // HEADS)


def attention_scores(queries, keys_all, same_seq):
    scale_factor = queries.shape[2] ** (-0.5)
    raw_scores = jnp.einsum("qhd,khd->hqk", queries, keys_all, preferred_element_type=jnp.float32)
    return jnp.where(same_seq[None], raw_scores * scale_factor, -1e30)


def mlp_products(pieces):
    active, grad_branch_m, normed_m, grad_upward = pieces[:4]
    grad_down_w = jnp.einsum("rf,rd->fd", active, grad_branch_m, preferred_element_type=jnp.float32)
    grad_in_w = jnp.einsum("rd,rf->df", normed_m, grad_upward, preferred_element_type=jnp.float32)
    return (grad_in_w, grad_down_w)


def attention_products(pieces):
    mixed, grad_branch_a, normed, grad_packed = pieces[4:]
    grad_out_w = jnp.einsum("rd,re->de", mixed, grad_branch_a, preferred_element_type=jnp.float32)
    grad_qkv_w = jnp.einsum("rd,re->de", normed, grad_packed, preferred_element_type=jnp.float32)
    return (grad_qkv_w, grad_out_w)


def layer_forward(hidden, modulation, same_seq, weights):
    w_qkv, w_out, w_in, w_down = weights
    row_count, feature_width = hidden.shape
    shift_a, scale_a, gate_a, shift_m, scale_m, gate_m = jnp.split(modulation, 6, axis=1)
    normed = modulate(hidden, shift_a, scale_a).astype(jnp.bfloat16)
    packed = low_dot(normed, w_qkv).astype(jnp.bfloat16)
    queries = split_heads(packed, 0)
    keys_all = split_heads(packed, 1)
    values_all = split_heads(packed, 2)
    scores = attention_scores(queries, keys_all, same_seq)
    row_peak = jnp.max(scores, axis=-1, keepdims=True)
    exponent = jnp.exp(scores - row_peak)
    row_total = jnp.sum(exponent, axis=-1, keepdims=True)
    probability = (exponent / row_total).astype(jnp.bfloat16)
    log_total = row_peak + jnp.log(row_total)
    mixed = jnp.einsum("hqk,khd->qhd", probability, values_all, preferred_element_type=jnp.float32)
    mixed = mixed.reshape(row_count, feature_width).astype(jnp.bfloat16)
    branch = low_dot(mixed, w_out)
    middle = hidden + gate_a * branch
    normed_m = modulate(middle, shift_m, scale_m).astype(jnp.bfloat16)
    upward = low_dot(normed_m, w_in)
    active = smooth_gate(upward).astype(jnp.bfloat16)
    output_branch = low_dot(active, w_down)
    result = middle + gate_m * output_branch
    kept_state = (
        hidden,
        normed,
        packed,
        log_total,
        mixed,
        branch,
        middle,
        normed_m,
        active,
        output_branch,
    )
    return (result, kept_state)


def layer_backward(grad_result, kept_state, modulation, same_seq, weights):
    w_qkv, w_out, w_in, w_down = weights
    hidden, normed, packed, log_total, mixed, branch, middle, normed_m, active, output_branch = (
        kept_state[:10]
    )
    upward = low_dot(normed_m, w_in)
    row_count, feature_width = hidden.shape
    shift_a, scale_a, gate_a, shift_m, scale_m, gate_m = jnp.split(modulation, 6, axis=1)
    grad_gate_m = grad_result * output_branch
    grad_branch_m = (gate_m * grad_result).astype(jnp.bfloat16)
    grad_active = jnp.einsum("rd,fd->rf", grad_branch_m, w_down, preferred_element_type=jnp.float32)
    unused_gate, gate_pull = jax.vjp(smooth_gate, upward)
    grad_upward = gate_pull(grad_active)[0].astype(jnp.bfloat16)
    grad_normed_m = jnp.einsum("rf,df->rd", grad_upward, w_in, preferred_element_type=jnp.float32)
    unused_middle, middle_pull = jax.vjp(modulate, middle, shift_m, scale_m)
    grad_middle, grad_shift_m, grad_scale_m = middle_pull(grad_normed_m)
    grad_middle = grad_middle + grad_result
    grad_gate_a = grad_middle * branch
    grad_branch_a = (gate_a * grad_middle).astype(jnp.bfloat16)
    grad_mixed = jnp.einsum("re,de->rd", grad_branch_a, w_out, preferred_element_type=jnp.float32)
    grad_mixed = grad_mixed.astype(jnp.bfloat16).reshape(row_count, HEADS, feature_width // HEADS)
    queries = split_heads(packed, 0)
    keys_all = split_heads(packed, 1)
    values_all = split_heads(packed, 2)
    scale_factor = queries.shape[2] ** (-0.5)
    scores = attention_scores(queries, keys_all, same_seq)
    probability = jnp.exp(scores - log_total)
    probability_low = probability.astype(jnp.bfloat16)
    grad_values = jnp.einsum(
        "hqk,qhd->khd", probability_low, grad_mixed, preferred_element_type=jnp.float32
    )
    grad_probability = jnp.einsum(
        "qhd,khd->hqk", grad_mixed, values_all, preferred_element_type=jnp.float32
    )
    inner_sum = jnp.sum(probability * grad_probability, axis=-1, keepdims=True)
    grad_scores = (probability * (grad_probability - inner_sum) * scale_factor).astype(jnp.bfloat16)
    grad_queries = jnp.einsum(
        "hqk,khd->qhd", grad_scores, keys_all, preferred_element_type=jnp.float32
    )
    grad_keys = jnp.einsum("hqk,qhd->khd", grad_scores, queries, preferred_element_type=jnp.float32)
    grad_packed = jnp.concatenate(
        [
            grad_queries.reshape(row_count, feature_width),
            grad_keys.reshape(row_count, feature_width),
            grad_values.reshape(row_count, feature_width),
        ],
        axis=1,
    ).astype(jnp.bfloat16)
    grad_normed = jnp.einsum("re,de->rd", grad_packed, w_qkv, preferred_element_type=jnp.float32)
    unused_hidden, hidden_pull = jax.vjp(modulate, hidden, shift_a, scale_a)
    grad_hidden, grad_shift_a, grad_scale_a = hidden_pull(grad_normed)
    grad_hidden = grad_hidden + grad_middle
    grad_modulation = jnp.concatenate(
        [grad_shift_a, grad_scale_a, grad_gate_a, grad_shift_m, grad_scale_m, grad_gate_m], axis=1
    )
    pieces = (
        active,
        grad_branch_m,
        normed_m,
        grad_upward,
        mixed,
        grad_branch_a,
        normed,
        grad_packed,
    )
    return (grad_hidden, pieces, grad_modulation)


def on_device(inputs, cotangent, long_count, timesteps, w_qkv, w_out, w_in, w_down, ada_weight):
    section_index = lax.axis_index("section")
    section_count = lax.axis_size("section")
    micro_count = long_count.shape[1]
    slot_count = timesteps.shape[2]
    feature_width = inputs.shape[1]
    row_count = inputs.shape[0] // micro_count
    tick_count = micro_count + section_count - 1
    weights = (w_qkv[0], w_out[0], w_in[0], w_down[0])
    first_flag = (section_index == 0).astype(jnp.float32)
    last_flag = (section_index == section_count - 1).astype(jnp.float32)
    input_rows = inputs.reshape(micro_count, row_count, feature_width)
    cot_rows = cotangent.reshape(micro_count, row_count, feature_width)
    features_low = time_features(timesteps[0].reshape(micro_count * slot_count)).astype(
        jnp.bfloat16
    )
    slot_features = features_low.astype(jnp.float32).reshape(
        micro_count, slot_count, features_low.shape[1]
    )
    mod_slots = low_dot(features_low, ada_weight[0]).reshape(
        micro_count, slot_count, 6 * feature_width
    )
    positions = jnp.arange(row_count, dtype=jnp.int32) // SHORT
    slot_ids = jnp.where(long_count[0][:, None] == 1, 0, positions[None, :])
    onehot = (
        slot_ids[:, :, None] == jnp.arange(slot_count, dtype=jnp.int32)[None, None, :]
    ).astype(jnp.float32)
    modulations = jnp.einsum("mrs,msc->mrc", onehot, mod_slots, precision=highest)
    same_seq = slot_ids[:, :, None] == slot_ids[:, None, :]

    def run_layer(hidden, picked):
        return layer_forward(hidden, modulations[picked], same_seq[picked], weights)

    def skip_layer(hidden, picked):
        return jax.tree.map(jnp.zeros_like, run_layer(hidden, picked))

    def run_back(grad_result, kept_state, picked):
        grad_hidden, pieces, grad_modulation = layer_backward(
            grad_result, kept_state, modulations[picked], same_seq[picked], weights
        )
        grad_slots = jnp.einsum("rs,rc->sc", onehot[picked], grad_modulation, precision=highest)
        grad_ada_w = jnp.einsum("st,sc->tc", slot_features[picked], grad_slots, precision=highest)
        grad_in_w, grad_down_w = mlp_products(pieces)
        grad_qkv_w, grad_out_w = attention_products(pieces)
        return (grad_hidden, (grad_qkv_w, grad_out_w, grad_in_w, grad_down_w, grad_ada_w))

    def skip_back(grad_result, kept_state, picked):
        return jax.tree.map(jnp.zeros_like, run_back(grad_result, kept_state, picked))

    received = jnp.zeros((row_count, feature_width), jnp.bfloat16)
    cond_rows = jnp.zeros((micro_count, row_count, feature_width), jnp.bfloat16)
    for tick_index in range(tick_count):
        batch_index = tick_index - section_index
        is_valid = (batch_index >= 0) & (batch_index < micro_count)
        picked = jnp.clip(batch_index, 0, micro_count - 1)
        target = jnp.where(is_valid, batch_index, micro_count)
        hidden = received.astype(jnp.float32) + first_flag * input_rows[picked].astype(jnp.float32)
        result = lax.cond(is_valid, run_layer, skip_layer, hidden, picked)[0].astype(jnp.bfloat16)
        cond_rows = place_row(cond_rows, target, result)
        if tick_index + 1 < tick_count:
            received = shifted(result, "section", 1)
    returned = shifted(cond_rows, "section", 1 - section_count)
    received = jnp.zeros((row_count, feature_width), jnp.bfloat16)
    main_rows = jnp.zeros((micro_count, row_count, feature_width), jnp.bfloat16)
    store = None
    for tick_index in range(tick_count):
        batch_index = tick_index - section_index
        is_valid = (batch_index >= 0) & (batch_index < micro_count)
        picked = jnp.clip(batch_index, 0, micro_count - 1)
        target = jnp.where(is_valid, batch_index, micro_count)
        start_here = input_rows[picked].astype(jnp.float32) + returned[picked].astype(jnp.float32)
        hidden = received.astype(jnp.float32) + first_flag * start_here
        result, kept_state = lax.cond(is_valid, run_layer, skip_layer, hidden, picked)
        if store is None:
            store = jax.tree.map(
                lambda piece: jnp.zeros((micro_count,) + piece.shape, piece.dtype), kept_state
            )
        store = jax.tree.map(
            lambda stored, piece: place_row(stored, target, piece), store, kept_state
        )
        result_low = result.astype(jnp.bfloat16)
        main_rows = place_row(main_rows, target, result_low)
        if tick_index + 1 < tick_count:
            received = shifted(result_low, "section", 1)
    received = jnp.zeros((row_count, feature_width), jnp.bfloat16)
    grad_rows = jnp.zeros((micro_count, row_count, feature_width), jnp.bfloat16)
    summed = None
    for tick_index in range(tick_count):
        batch_index = tick_index - (section_count - 1 - section_index)
        is_valid = (batch_index >= 0) & (batch_index < micro_count)
        picked = jnp.clip(batch_index, 0, micro_count - 1)
        target = jnp.where(is_valid, batch_index, micro_count)
        grad_result = received.astype(jnp.float32) + last_flag * cot_rows[picked].astype(
            jnp.float32
        )
        kept_state = jax.tree.map(lambda stored: stored[picked], store)
        grad_hidden, weight_side = lax.cond(
            is_valid, run_back, skip_back, grad_result, kept_state, picked
        )
        grad_low = grad_hidden.astype(jnp.bfloat16)
        grad_rows = place_row(grad_rows, target, grad_low)
        if summed is None:
            summed = weight_side
        else:
            summed = tuple(
                (left_term + right_term for left_term, right_term in zip(summed, weight_side))
            )
        if tick_index + 1 < tick_count:
            received = shifted(grad_low, "section", -1)
    summed = lax.psum_scatter(summed, "dp", scatter_dimension=0, tiled=True)
    hidden_out = main_rows.reshape(1, micro_count * row_count, feature_width)
    grad_in = grad_rows.reshape(1, micro_count * row_count, feature_width)
    return (
        hidden_out,
        grad_in,
        summed[0][None],
        summed[1][None],
        summed[2][None],
        summed[3][None],
        summed[4][None],
    )


def solution(mesh):
    placed = (
        P("dp", None),
        P("dp", None),
        P("dp", None),
        P("dp", None, None),
        P("section", None, None),
        P("section", None, None),
        P("section", None, None),
        P("section", None, None),
        P("section", None, None),
    )
    return jax.shard_map(
        on_device,
        mesh=mesh,
        in_specs=placed,
        out_specs=(
            P("section", "dp", None),
            P("section", "dp", None),
            P("section", "dp", None),
            P("section", "dp", None),
            P("section", "dp", None),
            P("section", "dp", None),
            P("section", "dp", None),
        ),
        check_vma=False,
    )
```

profile of v0, /device:TPU:0, one launch (start us, length us, event | category | flops | bytes accessed | tf_op | source)
XLA Modules:
  0.0 1384.6 jit_solution(16690359214172234515)
XLA Ops:
  17.7 22.7 %conditional.15 = (bf16[256,768]{1,0:T(8,128)(2,1)}) conditional(s32[]{:T(128)} %convert_element_type.840, () %tuple.537, (f32[]{:T(128)}, f32[256,768]{1,0:T(8,128)S(1)}, s32[]{:T(128)}, f32[2,256,4608]{2,1,0:T(8,128)}, bf16[768,2304]{1,0:T(8,128)(2,1)}, /*index=5*/pred[2,256,256]{1,2,0:T(8,128)(4,1)S(1)}, bf16[768,768]{1,0:T(8,128)(2,1)S(1)}, ...), branch_computations={%region_1.2_spmd, %region_2.9_spmd} | conditional | flops 3843490560 | bytes 82421880 | solution.py:239
  52.1 32.3 %conditional.16 = (bf16[256,768]{1,0:T(8,128)(2,1)}, bf16[1,256,768]{2,1,0:T(8,128)(2,1)S(1)}) conditional(s32[]{:T(128)} %convert_element_type.845, () %tuple.539, (f32[]{:T(128)}, f32[256,768]{1,0:T(8,128)}, f32[256,768]{1,0:T(8,128)}, s32[]{:T(128)}, f32[2,256,4608]{2,1,0:T(8,128)}, /*index=5*/bf16[768,2304]{1,0:T(8,128)(2,1)}, ...), branch_computations={%region_10.11_spmd, %region_11.18_spmd} | conditional | flops 3843097344 | bytes 87926936 | solution.py:239
  99.4 35.7 %collective-permute-start.2 = (bf16[256,768]{1,0:T(8,128)(2,1)}, bf16[256,768]{1,0:T(8,128)(2,1)S(1)}, u32[]{:S(2)}, u32[]{:S(2)}) collective-permute-start(bf16[256,768]{1,0:T(8,128)(2,1)} %get-tuple-element.2711), channel_id=1, source_target_pairs={{0,8},{8,16},{16,24},{1,9},{9,17},{17,25},{2,10},{10,18},{18,26},{... | collective-permute-start | bytes 1179656 | tf_op jit(solution)/shard_map/ppermute | solution.py:20
  164.8 77.0 %collective-permute-done.4 = bf16[2,256,768]{2,1,0:T(8,128)(2,1)S(1)} collective-permute-done((bf16[2,256,768]{2,1,0:T(8,128)(2,1)}, bf16[2,256,768]{2,1,0:T(8,128)(2,1)S(1)}, u32[]{:S(2)}, u32[]{:S(2)}) %collective-permute-start.4) | collective-permute-done | bytes 786464 | tf_op jit(solution)/shard_map/ppermute | solution.py:20
  242.7 42.3 %conditional.20 = (f32[256,768]{1,0:T(8,128)S(1)}, bf16[256,768]{1,0:T(8,128)(2,1)}, f32[256,768]{1,0:T(8,128)}, f32[256,768]{1,0:T(8,128)}, bf16[256,768]{1,0:T...) conditional(s32[]{:T(128)} %convert_element_type.840, ...), branch_computations={%region_45.46_spmd, %region_46.53_spmd} | conditional | flops 3848009216 | bytes 121817472 | solution.py:254
  321.3 49.0 %conditional.21 = (bf16[256,768]{1,0:T(8,128)(2,1)}, bf16[1,256,768]{2,1,0:T(8,128)(2,1)S(1)}, f32[1,256,768]{2,1,0:T(8,128)}, bf16[1,256,768]{2,1,0:T(8,128)(2,...) conditional(s32[]{:T(128)} %convert_element_type.845, ...), branch_computations={%region_53.54_spmd, %region_54.0_spmd} | conditional | flops 3855283712 | bytes 122341712 | solution.py:254
  395.0 9.7 conditional.22
  404.7 27.3 %collective-permute-start.7 = (bf16[256,768]{1,0:T(8,128)(2,1)}, bf16[256,768]{1,0:T(8,128)(2,1)S(1)}, u32[]{:S(2)}, u32[]{:S(2)}) collective-permute-start(bf16[256,768]{1,0:T(8,128)(2,1)} %get-tuple-element.2718), channel_id=1, source_target_pairs={{0,8},{8,16},{16,24},{1,9},{9,17},{17,25},{2,10},{10,18},{18,26},{... | collective-permute-start | bytes 1179656 | tf_op jit(solution)/shard_map/ppermute | solution.py:20
  496.7 10.0 conditional.24
  531.4 22.4 %conditional.25 = (f32[768,2304]{1,0:T(8,128)}, f32[768,768]{1,0:T(8,128)}, f32[768,3072]{1,0:T(8,128)}, f32[3072,768]{1,0:T(8,128)}, f32[128,4608]{1,0:T(8,128)...) conditional(s32[]{:T(128)} %convert_element_type.865, () %tuple.556, (s32[]{:T(128)}, ...), branch_computations={%region_91.92_spmd, %region_92.102_spmd} | conditional | flops 9046138880 | bytes 295677984 | solution.py:278
  555.1 27.1 %collective-permute-done.9 = bf16[256,768]{1,0:T(8,128)(2,1)} collective-permute-done((bf16[256,768]{1,0:T(8,128)(2,1)}, bf16[256,768]{1,0:T(8,128)(2,1)}, u32[]{:S(2)}, u32[]{:S(2)}) %collective-permute-start.9) | collective-permute-done | bytes 393248 | tf_op jit(solution)/shard_map/ppermute | solution.py:20
  584.1 22.6 %conditional.26 = (f32[768,2304]{1,0:T(8,128)}, f32[768,768]{1,0:T(8,128)}, f32[768,3072]{1,0:T(8,128)}, f32[3072,768]{1,0:T(8,128)}, f32[128,4608]{1,0:T(8,128)...) conditional(s32[]{:T(128)} %convert_element_type.869, () %tuple.558, (s32[]{:T(128)}, ...), branch_computations={%region_103.104_spmd, %region_104.114_spmd} | conditional | flops 9046138880 | bytes 295677984 | solution.py:278
  608.0 10.6 collective-permute-done.10
  620.5 22.7 %conditional.27 = (f32[768,2304]{1,0:T(8,128)}, f32[768,768]{1,0:T(8,128)}, f32[768,3072]{1,0:T(8,128)}, f32[3072,768]{1,0:T(8,128)}, f32[128,4608]{1,0:T(8,128)...) conditional(s32[]{:T(128)} %convert_element_type.871, () %tuple.560, (s32[]{:T(128)}, ...), branch_computations={%region_115.116_spmd, %region_116.126_spmd} | conditional | flops 9046138880 | bytes 295677984 | solution.py:278
  644.5 203.0 %collective-permute-done.11 = bf16[256,768]{1,0:T(8,128)(2,1)} collective-permute-done((bf16[256,768]{1,0:T(8,128)(2,1)}, bf16[256,768]{1,0:T(8,128)(2,1)}, u32[]{:S(2)}, u32[]{:S(2)}) %collective-permute-start.11) | collective-permute-done | bytes 393248 | tf_op jit(solution)/shard_map/ppermute | solution.py:20
  849.4 80.8 %conditional.28 = (f32[768,2304]{1,0:T(8,128)}, f32[768,768]{1,0:T(8,128)}, f32[768,3072]{1,0:T(8,128)}, f32[3072,768]{1,0:T(8,128)}, f32[128,4608]{1,0:T(8,128)...) conditional(s32[]{:T(128)} %convert_element_type.873, () %tuple.562, (s32[]{:T(128)}, ...), branch_computations={%region_127.128_spmd, %region_128.138_spmd} | conditional | flops 9046138880 | bytes 295677984 | solution.py:278
  931.5 9.6 collective-permute-done.12
  943.0 75.9 %conditional.29 = (f32[768,2304]{1,0:T(8,128)}, f32[768,768]{1,0:T(8,128)}, f32[768,3072]{1,0:T(8,128)}, f32[3072,768]{1,0:T(8,128)}, f32[128,4608]{1,0:T(8,128)S(1)}, /*index=5*/bf16[1,256,768]{2,1,0:T(8,128)(2,1)}) conditional(s32[]{:T(128)} %convert_element_type.875, () %tuple.564, (s32[]{:T(128)}, bf16[2,256,768]{2,1,0:T(8,128)(2,1)}, ...), branch_computations={%region_139.140_spmd, %region_140.150_spmd} | conditional | flops 9046138880 | bytes 293318656 | solution.py:278
  1031.9 15.6 %add_add_fusion.17 = f32[768,2304]{1,0:T(8,128)} fusion(f32[768,2304]{1,0:T(8,128)} %get-tuple-element.2785, f32[768,2304]{1,0:T(8,128)} %get-tuple-element.2784, f32[768,2304]{1,0:T(8,128)} %get-tuple-element.2783, f32[768,2304]{1,0:T(8,128)} %get-tuple-element.2781, f32[768,2304]{1,0:T(8,128)} %get-tuple-element.2782), kind=kLoop, calls=%fused_computation.1053 | loop fusion | flops 7077888 | bytes 42467328 | tf_op jit(solution)/shard_map/add | solution.py:287
  1047.5 20.7 %add_add_fusion.16 = f32[768,3072]{1,0:T(8,128)} fusion(f32[768,3072]{1,0:T(8,128)} %get-tuple-element.2795, f32[768,3072]{1,0:T(8,128)} %get-tuple-element.2794, f32[768,3072]{1,0:T(8,128)} %get-tuple-element.2793, f32[768,3072]{1,0:T(8,128)} %get-tuple-element.2791, f32[768,3072]{1,0:T(8,128)} %get-tuple-element.2792), kind=kLoop, calls=%fused_computation.1052 | loop fusion | flops 9437184 | bytes 56623104 | tf_op jit(solution)/shard_map/add | solution.py:287
  1068.3 19.9 %add_add_fusion.15 = f32[3072,768]{1,0:T(8,128)} fusion(f32[3072,768]{1,0:T(8,128)} %get-tuple-element.2800, f32[3072,768]{1,0:T(8,128)} %get-tuple-element.2799, f32[3072,768]{1,0:T(8,128)} %get-tuple-element.2798, f32[3072,768]{1,0:T(8,128)} %get-tuple-element.2796, f32[3072,768]{1,0:T(8,128)} %get-tuple-element.2797), kind=kLoop, calls=%fused_computation.1051 | loop fusion | flops 9437184 | bytes 56623104 | tf_op jit(solution)/shard_map/add | solution.py:287
  1097.2 79.3 %reduce-scatter.6.cloned.1.call-done = f32[96,2304]{1,0:T(8,128)} async-done(((f32[768,2304]{1,0:T(8,128)}), f32[96,2304]{1,0:T(8,128)}) %reduce-scatter.6.cloned.1.call-update) | async-done | bytes 884752 | tf_op jit(solution)/shard_map/reduce_scatter | solution.py:291
  1176.5 100.6 %reduce-scatter.10.cloned.1.call-done = f32[96,3072]{1,0:T(8,128)} async-done(((f32[768,3072]{1,0:T(8,128)}), f32[96,3072]{1,0:T(8,128)}) %reduce-scatter.10.cloned.1.call-update) | async-done | bytes 1179664 | tf_op jit(solution)/shard_map/reduce_scatter | solution.py:291
  1277.1 100.6 %reduce-scatter.12.cloned.1.call-done = f32[384,768]{1,0:T(8,128)} async-done(((f32[3072,768]{1,0:T(8,128)}), f32[384,768]{1,0:T(8,128)}) %reduce-scatter.12.cloned.1.call-update) | async-done | bytes 1179664 | tf_op jit(solution)/shard_map/reduce_scatter | solution.py:291
  (602 shorter events, 634.5 us)
Async XLA Ops:
  7.2 1090.0 %reduce-scatter.8.cloned.1.call-start = ((), (), s32[]{:S(2)}) async-start(), calls=%async_computation.6 | async-start | bytes 2654208 | tf_op jit(solution)/shard_map/reduce_scatter | solution.py:291
  8.9 232.9 %copy-start.38 = (pred[2,256,256]{1,2,0:T(8,128)(4,1)}, pred[2,256,256]{1,2,0:T(8,128)(4,1)S(1)}, u32[]{:S(2)}) copy-start(pred[2,256,256]{1,2,0:T(8,128)(4,1)S(1)} %broadcast_compare_fusion) | copy-start | bytes 393220
  40.4 10.9 collective-permute-start
  52.1 36.7 %copy-start.194 = (s32[3]{0:T(128)S(1)}, s32[3]{0:T(128)}, u32[]{:S(2)}) copy-start(s32[3]{0:T(128)} %constant.2365.clone.1) | copy-start | bytes 40
  84.5 13.0 collective-permute-start.1
  99.4 35.7 %copy-start.135 = (bf16[1,256,768]{2,1,0:T(8,128)(2,1)}, bf16[1,256,768]{2,1,0:T(8,128)(2,1)S(1)}, u32[]{:S(2)}) copy-start(bf16[1,256,768]{2,1,0:T(8,128)(2,1)S(1)} %get-tuple-element.2710) | copy-start | bytes 1179652
  99.4 43.5 %collective-permute-start.2 = (bf16[256,768]{1,0:T(8,128)(2,1)}, bf16[256,768]{1,0:T(8,128)(2,1)S(1)}, u32[]{:S(2)}, u32[]{:S(2)}) collective-permute-start(bf16[256,768]{1,0:T(8,128)(2,1)} %get-tuple-element.2711), channel_id=1, source_target_pairs={{0,8},{8,16},{16,24},{1,9},{9,17},{17,25},{2,10},{10,18},{18,26},{... | collective-permute-start | bytes 1179656 | tf_op jit(solution)/shard_map/ppermute | solution.py:20
  144.9 11.2 collective-permute-start.3
  160.1 81.8 %collective-permute-start.4 = (bf16[2,256,768]{2,1,0:T(8,128)(2,1)}, bf16[2,256,768]{2,1,0:T(8,128)(2,1)S(1)}, u32[]{:S(2)}, u32[]{:S(2)}) collective-permute-start(bf16[2,256,768]{2,1,0:T(8,128)(2,1)} %select_dynamic-update-slice_fusion.45), channel_id=1, source_target_pairs={{24,0},{25,1},{26,2},{27,3},{28,4},{29,5},{30,6},{31,7}} | collective-permute-start | bytes 2359304 | tf_op jit(solution)/shard_map/ppermute | solution.py:20
  286.0 34.3 %collective-permute-start.5 = (bf16[256,768]{1,0:T(8,128)(2,1)}, bf16[256,768]{1,0:T(8,128)(2,1)S(1)}, u32[]{:S(2)}, u32[]{:S(2)}) collective-permute-start(bf16[256,768]{1,0:T(8,128)(2,1)} %get-tuple-element.2714), channel_id=1, source_target_pairs={{0,8},{8,16},{16,24},{1,9},{9,17},{17,25},{2,10},{10,18},{18,26},{... | collective-permute-start | bytes 1179656 | tf_op jit(solution)/shard_map/ppermute | solution.py:20
  370.3 23.3 %collective-permute-start.6 = (bf16[256,768]{1,0:T(8,128)(2,1)}, bf16[256,768]{1,0:T(8,128)(2,1)S(1)}, u32[]{:S(2)}, u32[]{:S(2)}) collective-permute-start(bf16[256,768]{1,0:T(8,128)(2,1)} %get-tuple-element.2716), channel_id=1, source_target_pairs={{0,8},{8,16},{16,24},{1,9},{9,17},{17,25},{2,10},{10,18},{18,26},{... | collective-permute-start | bytes 1179656 | tf_op jit(solution)/shard_map/ppermute | solution.py:20
  404.7 51.0 %collective-permute-start.7 = (bf16[256,768]{1,0:T(8,128)(2,1)}, bf16[256,768]{1,0:T(8,128)(2,1)S(1)}, u32[]{:S(2)}, u32[]{:S(2)}) collective-permute-start(bf16[256,768]{1,0:T(8,128)(2,1)} %get-tuple-element.2718), channel_id=1, source_target_pairs={{0,8},{8,16},{16,24},{1,9},{9,17},{17,25},{2,10},{10,18},{18,26},{... | collective-permute-start | bytes 1179656 | tf_op jit(solution)/shard_map/ppermute | solution.py:20
  466.3 29.5 %collective-permute-start.8 = (bf16[256,768]{1,0:T(8,128)(2,1)}, bf16[256,768]{1,0:T(8,128)(2,1)S(1)}, u32[]{:S(2)}, u32[]{:S(2)}) collective-permute-start(bf16[256,768]{1,0:T(8,128)(2,1)} %get-tuple-element.2720), channel_id=1, source_target_pairs={{0,8},{8,16},{16,24},{1,9},{9,17},{17,25},{2,10},{10,18},{18,26},{... | collective-permute-start | bytes 1179656 | tf_op jit(solution)/shard_map/ppermute | solution.py:20
  553.8 28.4 %collective-permute-start.9 = (bf16[256,768]{1,0:T(8,128)(2,1)}, bf16[256,768]{1,0:T(8,128)(2,1)}, u32[]{:S(2)}, u32[]{:S(2)}) collective-permute-start(bf16[256,768]{1,0:T(8,128)(2,1)} %get-tuple-element.2773), channel_id=1, source_target_pairs={{8,0},{16,8},{24,16},{9,1},{17,9},{25,17},{10,2},{18,10},{26,18},{... | collective-permute-start | bytes 1179656 | tf_op jit(solution)/shard_map/ppermute | solution.py:20
  606.7 11.9 collective-permute-start.10
  643.2 204.3 %collective-permute-start.11 = (bf16[256,768]{1,0:T(8,128)(2,1)}, bf16[256,768]{1,0:T(8,128)(2,1)}, u32[]{:S(2)}, u32[]{:S(2)}) collective-permute-start(bf16[256,768]{1,0:T(8,128)(2,1)} %get-tuple-element.2777), channel_id=1, source_target_pairs={{8,0},{16,8},{24,16},{9,1},{17,9},{25,17},{10,2},{18,10},{26,18},{... | collective-permute-start | bytes 1179656 | tf_op jit(solution)/shard_map/ppermute | solution.py:20
  930.2 10.9 collective-permute-start.12
  1025.5 71.7 %reduce-scatter.14.cloned.1.call-start = ((), (), s32[]{:S(2)}) async-start(), calls=%async_computation.9 | async-start | bytes 2654208 | tf_op jit(solution)/shard_map/reduce_scatter | solution.py:291
  1031.8 144.7 %reduce-scatter.6.cloned.1.call-start = ((), (), s32[]{:S(2)}) async-start(), calls=%async_computation.5 | async-start | bytes 7962624 | tf_op jit(solution)/shard_map/reduce_scatter | solution.py:291
  1047.5 229.7 %reduce-scatter.10.cloned.1.call-start = ((), (), s32[]{:S(2)}) async-start(), calls=%async_computation.7 | async-start | bytes 10616832 | tf_op jit(solution)/shard_map/reduce_scatter | solution.py:291
  1068.2 309.5 %reduce-scatter.12.cloned.1.call-start = ((), (), s32[]{:S(2)}) async-start(), calls=%async_computation.8 | async-start | bytes 10616832 | tf_op jit(solution)/shard_map/reduce_scatter | solution.py:291
  1092.1 285.7 %copy-start.69 = (bf16[2,256,768]{2,1,0:T(8,128)(2,1)}, bf16[2,256,768]{2,1,0:T(8,128)(2,1)S(1)}, u32[]{:S(2)}) copy-start(bf16[2,256,768]{2,1,0:T(8,128)(2,1)S(1)} %select_dynamic-update-slice_fusion.41) | copy-start | bytes 2359300
  1092.1 285.7 %copy-start.1 = (bf16[1,128,4608]{2,1,0:T(8,128)(2,1)S(1)}, bf16[1,128,4608]{2,1,0:T(8,128)(2,1)}, u32[]{:S(2)}) copy-start(bf16[1,128,4608]{2,1,0:T(8,128)(2,1)} %param.177) | copy-start | bytes 3538948
  1097.1 280.7 %copy-start.63 = (bf16[2,256,768]{2,1,0:T(8,128)(2,1)}, bf16[2,256,768]{2,1,0:T(8,128)(2,1)S(1)}, u32[]{:S(2)}) copy-start(bf16[2,256,768]{2,1,0:T(8,128)(2,1)S(1)} %select_dynamic-update-slice_fusion.24) | copy-start | bytes 2359300
  (108 other events, 515.6 us)
Sparse Core Ops, SparseCore 0:
  1025.6 33.0 reduce-scatter.7
  1061.6 35.4 reduce-scatter.13
  1100.0 76.4 reduce-scatter.5
  1179.2 97.8 reduce-scatter.9
  1279.9 97.8 reduce-scatter.11
where the time goes:
time: 1400 us; the launch traced here: 1380 us
  waiting for transfers between devices  631 us (45%)
  other arithmetic  266 us (19%)
  matrix products  195 us (14%)
  local copies, waits for them, and re-layouts  170 us (12%)
  starting transfers between devices  87.9 us (6%)
  loops' own time  20.4 us (1%)
  between operations  14.9 us (1%)
    ppermute x13, waiting for transfers between devices, shifted(): return lax.ppermute(block, axis, route)  350 us
    reduce_scatter x5, waiting for transfers between devices, on_device(): summed = lax.psum_scatter(summed, 'dp', scatter_dimension=0, tiled=True)  281 us
    scatter x61, other arithmetic, place_row(): return buffer.at[target].set(piece, mode='drop')  134 us
    ppermute x13, starting transfers between devices, shifted(): return lax.ppermute(block, axis, route)  87.7 us
    another operation x72, local copies, waits for them, and re-layouts  87.3 us
    add x5, other arithmetic, on_device(): left_term + right_term  69.1 us
    dot_general x17, matrix products, low_dot(): return jnp.dot(left_side, right_side, preferred_element_type=jnp.float32)  61.1 us
  transfers between devices with their start and end apart: 18, of which 12 were waited for; matrix products, arithmetic and copies ran while one was open for 13% of the time, Pallas kernels for 0%

commit v1 on v0

v1 whole, which is shorter than its diff:
```python
import functools
import math

import jax
import jax.numpy as jnp
from jax import lax
from jax.experimental import pallas as pl
from jax.experimental.pallas import tpu as pltpu
from jax.sharding import PartitionSpec as P

HEADS = 12
TEMB = 128
SHORT = 128
TILE = 256
CHUNK = 32
norm_eps = 1e-06
MESH = pl.DeviceIdType.MESH
low = jnp.bfloat16
wide = jnp.float32


def dot_nn(a, b):
    return lax.dot_general(a, b, (((1,), (0,)), ((), ())), preferred_element_type=wide)


def dot_nt(a, b):
    return lax.dot_general(a, b, (((1,), (1,)), ((), ())), preferred_element_type=wide)


def dot_tn(a, b):
    return lax.dot_general(a, b, (((0,), (0,)), ((), ())), preferred_element_type=wide)


def fold(block):
    total = block[0:8]
    for start in range(8, block.shape[0], 8):
        total = total + block[start : start + 8]
    return total


GELU_C = math.sqrt(2.0 / math.pi)


def gelu(u):
    t = jnp.tanh(GELU_C * (u + 0.044715 * (u * u * u)))
    return 0.5 * u * (1.0 + t)


def gelu_slope(u):
    square = u * u
    t = jnp.tanh(GELU_C * (u + 0.044715 * (square * u)))
    return 0.5 * (1.0 + t) + 0.5 * u * (1.0 - t * t) * (GELU_C * (1.0 + (3.0 * 0.044715) * square))


def chain_kernel(
    sections,
    x_ref,
    cot_ref,
    mod_ref,
    bias_ref,
    wqkv_ref,
    wout_ref,
    win_ref,
    wdown_ref,
    fout_ref,
    gin_ref,
    dmod_ref,
    a1_ref,
    qkv_ref,
    o_ref,
    dattn_ref,
    a2_ref,
    du_ref,
    z_ref,
    dy_ref,
    h_s,
    m_s,
    t_s,
    do_s,
    n1_s,
    n2_s,
    r1_s,
    r2_s,
    y_s,
    frecv,
    brecv,
    fss,
    frs,
    bss,
    brs,
):
    micro, rows, width = x_ref.shape
    ff = win_ref.shape[1]
    half_rows = SHORT
    chunks = [(start, start // half_rows) for start in range(0, rows, CHUNK)]
    halves = rows // half_rows
    section = lax.axis_index("section")
    member = lax.axis_index("dp")
    right = lax.rem(section + 1, sections)
    left = lax.rem(section + sections - 1, sections)
    is_first = section == 0
    is_last = section == sections - 1

    barrier = pltpu.get_barrier_semaphore()
    for neighbour in (left, right):
        pl.semaphore_signal(barrier, inc=1, device_id=(neighbour, member), device_id_type=MESH)
    pl.semaphore_wait(barrier, 2)

    def forward_copy(job, slot):
        return pltpu.make_async_remote_copy(
            src_ref=fout_ref.at[job],
            dst_ref=frecv.at[slot],
            send_sem=fss.at[job],
            recv_sem=frs.at[slot],
            device_id=(right, member),
            device_id_type=MESH,
        )

    def backward_copy(job):
        return pltpu.make_async_remote_copy(
            src_ref=gin_ref.at[job],
            dst_ref=brecv.at[job],
            send_sem=bss.at[job],
            recv_sem=brs.at[job],
            device_id=(left, member),
            device_id_type=MESH,
        )

    def mod_row(mb, half, k):
        return mod_ref[mb, half, pl.ds(k, 1), :]

    lane = lax.broadcasted_iota(jnp.int32, (1, 128), 1)
    first_lanes = lane < 64
    masks = [first_lanes.astype(wide).astype(low), (1.0 - first_lanes.astype(wide)).astype(low)]
    scale = (width // HEADS) ** (-0.5)

    def norm_forward(src, mb, k_shift, k_scale, n_keep, r_keep, out):
        for start, half in chunks:
            span = pl.ds(start, CHUNK)
            v = src[span, :]
            centered = v - jnp.mean(v, axis=-1, keepdims=True)
            r = lax.rsqrt(jnp.mean(centered * centered, axis=-1, keepdims=True) + norm_eps)
            n = centered * r
            n_keep[mb, span, :] = n.astype(low)
            r_keep[mb, span, :] = r
            out[mb, span, :] = (
                n * (1.0 + mod_row(mb, half, k_scale)) + mod_row(mb, half, k_shift)
            ).astype(low)

    def forward_job(job, carry):
        mb = lax.rem(job, micro)

        @pl.when(jnp.logical_or(jnp.logical_not(is_first), job >= micro))
        def _():
            forward_copy(job, job).wait_recv()

        @pl.when(jnp.logical_and(is_first, job < micro))
        def _():
            h_s[...] = x_ref[mb].astype(wide)

        @pl.when(jnp.logical_and(is_first, job >= micro))
        def _():
            h_s[...] = x_ref[mb].astype(wide) + frecv[job].astype(wide)

        @pl.when(jnp.logical_not(is_first))
        def _():
            h_s[...] = frecv[job].astype(wide)

        norm_forward(h_s, mb, 0, 1, n1_s, r1_s, a1_ref)
        a1 = a1_ref[mb]
        for c in range(0, 3 * width, TILE):
            qkv_ref[mb, :, c : c + TILE] = dot_nn(a1, wqkv_ref[:, c : c + TILE]).astype(low)
        bias = bias_ref[mb]
        for c in range(0, width, 128):
            q = qkv_ref[mb, :, c : c + 128]
            k = qkv_ref[mb, :, width + c : width + c + 128]
            v = qkv_ref[mb, :, 2 * width + c : 2 * width + c + 128]
            outs = []
            for mask in masks:
                s = dot_nt(q * (mask * scale), k) + bias
                e = jnp.exp(s - jnp.max(s, axis=1, keepdims=True))
                p = (e * (1.0 / jnp.sum(e, axis=1, keepdims=True))).astype(low)
                outs.append(dot_nn(p, v))
            o_ref[mb, :, c : c + 128] = jnp.where(first_lanes, outs[0], outs[1]).astype(low)
        o = o_ref[mb]
        for c in range(0, width, TILE):
            t_s[:, c : c + TILE] = dot_nn(o, wout_ref[:, c : c + TILE])
        for start, half in chunks:
            span = pl.ds(start, CHUNK)
            attn = t_s[span, :]
            dattn_ref[mb, span, :] = attn.astype(low)
            m_s[span, :] = h_s[span, :] + mod_row(mb, half, 2) * attn
        norm_forward(m_s, mb, 3, 4, n2_s, r2_s, a2_ref)
        a2 = a2_ref[mb]
        for c in range(0, ff, TILE):
            u = dot_nn(a2, win_ref[:, c : c + TILE])
            du_ref[mb, :, c : c + TILE] = u.astype(low)
            z_ref[mb, :, c : c + TILE] = gelu(u).astype(low)
        z = z_ref[mb]
        for c in range(0, width, TILE):
            t_s[:, c : c + TILE] = dot_nn(z, wdown_ref[:, c : c + TILE])
        for start, half in chunks:
            span = pl.ds(start, CHUNK)
            y = t_s[span, :]
            y_s[mb, span, :] = y.astype(low)
            fout_ref[job, span, :] = (m_s[span, :] + mod_row(mb, half, 5) * y).astype(low)

        @pl.when(jnp.logical_or(jnp.logical_not(is_last), job < micro))
        def _():
            forward_copy(job, jnp.where(is_last, job + micro, job)).start()

        return carry

    lax.fori_loop(0, 2 * micro, forward_job, 0)

    def norm_backward(mb, k_scale, n_keep, r_keep, base, per_chunk):
        for half in range(halves):
            shift_sum = jnp.zeros((8, width), wide)
            scale_sum = jnp.zeros((8, width), wide)
            gate_sum = jnp.zeros((8, width), wide)
            for start in range(half * half_rows, (half + 1) * half_rows, CHUNK):
                span = pl.ds(start, CHUNK)
                da = t_s[span, :]
                n = n_keep[mb, span, :].astype(wide)
                r = r_keep[mb, span, :]
                shift_sum = shift_sum + fold(da)
                scale_sum = scale_sum + fold(da * n)
                dn = da * (1.0 + mod_row(mb, half, k_scale))
                dv = r * (
                    dn
                    - jnp.mean(dn, axis=-1, keepdims=True)
                    - n * jnp.mean(dn * n, axis=-1, keepdims=True)
                )
                extra = per_chunk(span, half, base[span, :] + dv)
                if extra is not None:
                    gate_sum = gate_sum + fold(extra)
            dmod_ref[mb, half, k_scale - 1, :] = jnp.sum(shift_sum, axis=0)
            dmod_ref[mb, half, k_scale, :] = jnp.sum(scale_sum, axis=0)
            if k_scale == 4:
                dmod_ref[mb, half, 2, :] = jnp.sum(gate_sum, axis=0)

    def backward_job(mb, carry):
        g_s = h_s

        @pl.when(is_last)
        def _():
            g_s[...] = cot_ref[mb].astype(wide)

        @pl.when(jnp.logical_not(is_last))
        def _():
            backward_copy(mb).wait_recv()
            g_s[...] = brecv[mb].astype(wide)

        for half in range(halves):
            gate_sum = jnp.zeros((8, width), wide)
            for start in range(half * half_rows, (half + 1) * half_rows, CHUNK):
                span = pl.ds(start, CHUNK)
                g = g_s[span, :]
                gate_sum = gate_sum + fold(g * y_s[mb, span, :].astype(wide))
                dy_ref[mb, span, :] = (mod_row(mb, half, 5) * g).astype(low)
            dmod_ref[mb, half, 5, :] = jnp.sum(gate_sum, axis=0)
        dy = dy_ref[mb]
        for c in range(0, ff, TILE):
            dz = dot_nt(dy, wdown_ref[c : c + TILE, :])
            u = du_ref[mb, :, c : c + TILE].astype(wide)
            du_ref[mb, :, c : c + TILE] = (gelu_slope(u) * dz).astype(low)
        du = du_ref[mb]
        for c in range(0, width, TILE):
            t_s[:, c : c + TILE] = dot_nt(du, win_ref[c : c + TILE, :])

        def after_mlp(span, half, dm):
            m_s[span, :] = dm
            extra = dm * dattn_ref[mb, span, :].astype(wide)
            dattn_ref[mb, span, :] = (mod_row(mb, half, 2) * dm).astype(low)
            return extra

        norm_backward(mb, 4, n2_s, r2_s, g_s, after_mlp)
        dattn = dattn_ref[mb]
        for c in range(0, width, TILE):
            do_s[:, c : c + TILE] = dot_nt(dattn, wout_ref[c : c + TILE, :]).astype(low)
        bias = bias_ref[mb]
        for c in range(0, width, 128):
            cols = [slice(i * width + c, i * width + c + 128) for i in range(3)]
            q, k, v = [qkv_ref[mb, :, cut] for cut in cols]
            do = do_s[:, c : c + 128]
            parts = []
            for mask in masks:
                s = dot_nt(k, q * (mask * scale)) + bias
                e = jnp.exp(s - jnp.max(s, axis=0, keepdims=True))
                p = e * (1.0 / jnp.sum(e, axis=0, keepdims=True))
                dp = dot_nt(v * mask, do)
                inner = jnp.sum(p * dp, axis=0, keepdims=True)
                ds = (p * (dp - inner) * scale).astype(low)
                parts.append((dot_tn(ds, k), dot_nn(ds, q), dot_nn(p.astype(low), do)))
            for i in range(3):
                qkv_ref[mb, :, cols[i]] = jnp.where(
                    first_lanes, parts[0][i], parts[1][i]
                ).astype(low)
        dqkv = qkv_ref[mb]
        for c in range(0, width, TILE):
            t_s[:, c : c + TILE] = dot_nt(dqkv, wqkv_ref[c : c + TILE, :])

        def after_attention(span, half, dh):
            gin_ref[mb, span, :] = dh.astype(low)

        norm_backward(mb, 1, n1_s, r1_s, m_s, after_attention)

        @pl.when(jnp.logical_not(is_first))
        def _():
            backward_copy(mb).start()

        return carry

    lax.fori_loop(0, micro, backward_job, 0)

    for job in range(2 * micro):

        @pl.when(jnp.logical_or(jnp.logical_not(is_last), job < micro))
        def _():
            forward_copy(job, job).wait_send()

    for job in range(micro):

        @pl.when(jnp.logical_not(is_first))
        def _():
            backward_copy(job).wait_send()


def run_chain(x, cot, mod, bias, w_qkv, w_out, w_in, w_down):
    micro, rows, width = x.shape
    ff = w_in.shape[1]
    sections = lax.axis_size("section")
    vmem = pl.BlockSpec(memory_space=pltpu.VMEM)

    def kept(columns):
        return jax.ShapeDtypeStruct((micro, rows, columns), low)

    out_shape = (
        jax.ShapeDtypeStruct((2 * micro, rows, width), low),
        kept(width),
        jax.ShapeDtypeStruct(mod.shape, wide),
        kept(width),
        kept(3 * width),
        kept(width),
        kept(width),
        kept(width),
        kept(ff),
        kept(ff),
        kept(width),
    )
    scratch = [
        pltpu.VMEM((rows, width), wide),
        pltpu.VMEM((rows, width), wide),
        pltpu.VMEM((rows, width), wide),
        pltpu.VMEM((rows, width), low),
        pltpu.VMEM((micro, rows, width), low),
        pltpu.VMEM((micro, rows, width), low),
        pltpu.VMEM((micro, rows, 1), wide),
        pltpu.VMEM((micro, rows, 1), wide),
        pltpu.VMEM((micro, rows, width), low),
        pltpu.VMEM((2 * micro, rows, width), low),
        pltpu.VMEM((micro, rows, width), low),
        pltpu.SemaphoreType.DMA((2 * micro,)),
        pltpu.SemaphoreType.DMA((2 * micro,)),
        pltpu.SemaphoreType.DMA((micro,)),
        pltpu.SemaphoreType.DMA((micro,)),
    ]
    return pl.pallas_call(
        functools.partial(chain_kernel, sections),
        out_shape=out_shape,
        in_specs=[vmem] * 8,
        out_specs=(vmem,) * len(out_shape),
        scratch_shapes=scratch,
        compiler_params=pltpu.CompilerParams(
            collective_id=0, has_side_effects=True, vmem_limit_bytes=60 * 1024 * 1024
        ),
    )(x, cot, mod, bias, w_qkv, w_out, w_in, w_down)


def time_features(timestep_ids):
    half_width = TEMB // 2
    frequency = jnp.exp(-math.log(10000.0) * jnp.arange(half_width, dtype=wide) / half_width)
    angles = timestep_ids.astype(wide)[:, None] * 0.1 * frequency[None, :]
    return jnp.concatenate([jnp.sin(angles), jnp.cos(angles)], axis=1)


def on_device(inputs, cotangent, long_count, timesteps, w_qkv, w_out, w_in, w_down, ada_weight):
    micro = long_count.shape[1]
    width = inputs.shape[1]
    rows = inputs.shape[0] // micro
    halves = rows // SHORT
    is_long = (long_count[0] == 1)[:, None]
    half_index = jnp.arange(halves, dtype=jnp.int32)[None, :]
    half_steps = jnp.where(is_long, timesteps[0][:, :1], timesteps[0][:, :halves])
    features = time_features(half_steps.reshape(-1)).astype(low)
    mod = jnp.dot(features, ada_weight[0], preferred_element_type=wide)
    mod = mod.reshape(micro, halves, 6, width)
    mod = jnp.pad(mod, ((0, 0), (0, 0), (0, 2), (0, 0)))
    slot_ids = jnp.where(is_long, 0, jnp.repeat(half_index, SHORT, axis=1))
    same = slot_ids[:, :, None] == slot_ids[:, None, :]
    bias = jnp.where(same, 0.0, -1e30).astype(wide)
    fout, gin, dmod, a1, dqkv, o, dattn, a2, du, z, dy = run_chain(
        inputs.reshape(micro, rows, width),
        cotangent.reshape(micro, rows, width),
        mod,
        bias,
        w_qkv[0],
        w_out[0],
        w_in[0],
        w_down[0],
    )

    def product(left, right):
        left = left.reshape(micro * rows, left.shape[2])
        right = right.reshape(micro * rows, right.shape[2])
        partial = dot_tn(left, right).astype(low)
        return lax.psum_scatter(partial, "dp", scatter_dimension=0, tiled=True).astype(wide)

    grad_down = product(z, dy)
    grad_up = product(a2, du)
    grad_out = product(o, dattn)
    grad_qkv = product(a1, dqkv)
    features_all = lax.all_gather(features.astype(wide), "dp", tiled=True)
    dmod_all = lax.all_gather(
        dmod[:, :, :6].reshape(micro * halves, 6 * width), "dp", tiled=True
    )
    share = TEMB // lax.axis_size("dp")
    mine = lax.dynamic_slice_in_dim(features_all, lax.axis_index("dp") * share, share, 1)
    grad_ada = lax.dot_general(
        mine, dmod_all, (((0,), (0,)), ((), ())), precision=lax.Precision.HIGHEST
    )
    hidden_out = fout[micro:].reshape(1, micro * rows, width)
    grad_in = gin.reshape(1, micro * rows, width)
    return (
        hidden_out,
        grad_in,
        grad_qkv[None],
        grad_out[None],
        grad_up[None],
        grad_down[None],
        grad_ada[None],
    )


def solution(mesh):
    placed = (
        P("dp", None),
        P("dp", None),
        P("dp", None),
        P("dp", None, None),
        P("section", None, None),
        P("section", None, None),
        P("section", None, None),
        P("section", None, None),
        P("section", None, None),
    )
    return jax.shard_map(
        on_device,
        mesh=mesh,
        in_specs=placed,
        out_specs=(P("section", "dp", None),) * 7,
        check_vma=False,
    )
```

time: 1400 us -> 439 us (0.31); the launches traced: 1380 us -> 438 us
  waiting for transfers between devices: 631 us -> 129 us
  other arithmetic: 266 us -> 10.7 us
  Pallas kernels: 0 us -> 223 us
  matrix products: 195 us -> 23.3 us
  local copies, waits for them, and re-layouts: 170 us -> 8.74 us
  starting transfers between devices: 87.9 us -> 0.38 us
  blocking collectives: 0 us -> 29.3 us
  loops' own time: 20.4 us -> 0 us
    ppermute x13 -> x0, waiting for transfers between devices: 350 us -> none  [shifted(): return lax.ppermute(block, axis, route)]
    pallas_call x0 -> x1, Pallas kernels: none -> 223 us  [run_chain(): pl.pallas_call(functools.partial(chain_kernel, sections), out_shape=out_s...]
    dot_general x54 -> x6, matrix products: 187 us -> 23.3 us  [the longest x4 21.6 us: dot_tn(): lax.dot_general(a, b, (((0,), (0,)), ((), ())), preferred_element_type=wide)]
    reduce_scatter x5 -> x4, waiting for transfers between devices: 281 us -> 129 us  [product(): lax.psum_scatter(partial, 'dp', scatter_dimension=0, tiled=True)]
    scatter x61 -> x0, other arithmetic: 134 us -> none  [place_row(): return buffer.at[target].set(piece, mode='drop')]
    ppermute x13 -> x0, starting transfers between devices: 87.7 us -> none  [shifted(): return lax.ppermute(block, axis, route)]
    another operation x72 -> x0, local copies, waits for them, and re-layouts: 87.3 us -> none
    add x7 -> x0, other arithmetic: 69.1 us -> none  [the longest x5 69.1 us: on_device(): left_term + right_term]
  transfers between devices with their start and end apart: 18 -> 4, of which waited for: 12 -> 3; matrix products, arithmetic and copies ran while one was open for 13% -> 6% of each run, Pallas kernels for 0% -> 0%
where the time goes in v1:
time: 439 us; the launch traced here: 438 us
  Pallas kernels  223 us (51%)
  waiting for transfers between devices  129 us (29%)
  blocking collectives  29.3 us (7%)
  matrix products  23.3 us (5%)
  between operations  13.9 us (3%)
  other arithmetic  10.7 us (2%)
  local copies, waits for them, and re-layouts  8.74 us (2%)
    pallas_call x1, Pallas kernels, run_chain(): pl.pallas_call(functools.partial(chain_kernel, sections), out_shape=out_s...  223 us
    reduce_scatter x4, waiting for transfers between devices, product(): lax.psum_scatter(partial, 'dp', scatter_dimension=0, tiled=True)  129 us
    dot_general x4, matrix products, dot_tn(): lax.dot_general(a, b, (((0,), (0,)), ((), ())), preferred_element_type=wide)  21.6 us
    all_gather x1, blocking collectives, on_device(): lax.all_gather(dmod[:, :, :6].reshape(micro * halves, 6 * width), 'dp', t...  15.8 us
    all_gather x1, blocking collectives, on_device(): features_all = lax.all_gather(features.astype(wide), 'dp', tiled=True)  13.5 us
  transfers between devices with their start and end apart: 4, of which 3 were waited for; matrix products, arithmetic and copies ran while one was open for 6% of the time, Pallas kernels for 0%

profile of v1, /device:TPU:0, one launch (start us, length us, event | category | flops | bytes accessed | tf_op | source)
XLA Modules:
  0.0 438.2 jit_solution(12150822266058221096)
XLA Ops:
  7.2 0.7 compare_bitcast_fusion
  7.9 0.8 slice_reduce_fusion
  8.7 0.8 convert_multiply_fusion
  9.5 0.9 compare_select_fusion.bias_ref
  10.5 1.7 copy.28
  13.4 222.7 %shard_map.144 = (bf16[4,256,768]{2,1,0:T(8,128)(2,1)}, bf16[2,256,768]{2,1,0:T(8,128)(2,1)}, f32[2,2,8,768]{3,2,1,0:T(8,128)}, bf16[2,256,768]{2,1,0:T(8,128)(2...) custom-call(bf16[2,256,768]{2,1,0:T(8,128)(2,1)} %bitcast.70, ...), custom_call_target="tpu_custom_call" | custom-call | tf_op jit(solution)/shard_map/pallas_call | solution.py:368
  236.2 3.3 bitcast_convert_fusion.3
  239.7 5.5 %bitcast_convert_fusion.2 = bf16[768,2304]{1,0:T(8,128)(2,1)} fusion(bf16[2,256,768]{2,1,0:T(8,128)(2,1)S(1)} %copy-done.6, bf16[2,256,2304]{2,1,0:T(8,128)(2,1)} %get-tuple-element.21), kind=kOutput, calls=%fused_computation.2 | convolution fusion | flops 1813708800 | bytes 6684672 | tf_op jit(solution)/shard_map/dot_general | solution.py:31
  245.3 1.1 copy-done.5
  246.4 6.2 %bitcast_convert_fusion.1 = bf16[768,3072]{1,0:T(8,128)(2,1)} fusion(bf16[2,256,768]{2,1,0:T(8,128)(2,1)S(1)} %copy-done.5, bf16[2,256,3072]{2,1,0:T(8,128)(2,1)} %get-tuple-element.25), kind=kOutput, calls=%fused_computation.1 | convolution fusion | flops 2418278400 | bytes 8650752 | tf_op jit(solution)/shard_map/dot_general | solution.py:31
  252.6 1.1 copy-done.4
  253.7 6.7 %bitcast_convert_fusion = bf16[3072,768]{1,0:T(8,128)(2,1)} fusion(bf16[2,256,3072]{2,1,0:T(8,128)(2,1)} %get-tuple-element.26, bf16[2,256,768]{2,1,0:T(8,128)(2,1)S(1)} %copy-done.4), kind=kOutput, calls=%fused_computation | convolution fusion | flops 2418278400 | bytes 8650752 | tf_op jit(solution)/shard_map/dot_general | solution.py:31
  261.8 0.9 slice.10
  262.8 15.8 %all-gather.1 = f32[8,4,4608]{2,1,0:T(4,128)S(1)} all-gather(f32[1,4,4608]{2,1,0:T(4,128)S(1)} %reshape.157), channel_id=1, replica_groups=mesh['section'=4,'dp'=8] {'dp'}, dimensions={0}, use_global_device_ids=true | all-gather | bytes 663552 | tf_op jit(solution)/shard_map/all_gather | solution.py:424
  279.0 13.5 %all-gather = f32[8,4,128]{2,1,0:T(4,128)S(1)} all-gather(f32[1,4,128]{2,1,0:T(4,128)S(1)} %fusion.8), channel_id=1, replica_groups=mesh['section'=4,'dp'=8] {'dp'}, dimensions={0}, use_global_device_ids=true | all-gather | bytes 18432 | tf_op jit(solution)/shard_map/all_gather | solution.py:423
  292.5 1.3 convolution_bitcast_fusion
  293.8 1.6 bitcast_convert_fusion.7
  295.4 21.8 %reduce-scatter.5.cloned.1.call-done = bf16[96,2304]{1,0:T(8,128)(2,1)} async-done(((bf16[768,2304]{1,0:T(8,128)(2,1)}), bf16[96,2304]{1,0:T(8,128)(2,1)}) %reduce-scatter.5.cloned.1.call-update) | async-done | bytes 442384 | tf_op jit(solution)/shard_map/reduce_scatter | solution.py:417
  317.2 2.0 bitcast_convert_fusion.6
  319.2 53.8 %reduce-scatter.9.cloned.1.call-done = bf16[96,3072]{1,0:T(8,128)(2,1)} async-done(((bf16[768,3072]{1,0:T(8,128)(2,1)}), bf16[96,3072]{1,0:T(8,128)(2,1)}) %reduce-scatter.9.cloned.1.call-update) | async-done | bytes 589840 | tf_op jit(solution)/shard_map/reduce_scatter | solution.py:417
  373.0 2.2 bitcast_convert_fusion.5
  375.1 53.5 %reduce-scatter.11.cloned.1.call-done = bf16[384,768]{1,0:T(8,128)(2,1)} async-done(((bf16[3072,768]{1,0:T(8,128)(2,1)}), bf16[384,768]{1,0:T(8,128)(2,1)}) %reduce-scatter.11.cloned.1.call-update) | async-done | bytes 589840 | tf_op jit(solution)/shard_map/reduce_scatter | solution.py:417
  428.6 2.2 bitcast_convert_fusion.4
  430.8 0.9 copy.40
  (38 shorter events, 3.6 us)
Async XLA Ops:
  7.2 286.6 %reduce-scatter.7.cloned.1.call-start = ((), (), s32[]{:S(2)}) async-start(), calls=%async_computation.5 | async-start | bytes 1327104 | tf_op jit(solution)/shard_map/reduce_scatter | solution.py:417
  236.2 3.6 copy-start.6
  239.5 77.7 %reduce-scatter.5.cloned.1.call-start = ((), (), s32[]{:S(2)}) async-start(), calls=%async_computation.4 | async-start | bytes 3981312 | tf_op jit(solution)/shard_map/reduce_scatter | solution.py:417
  245.2 1.1 copy-start.5
  245.3 127.7 %reduce-scatter.9.cloned.1.call-start = ((), (), s32[]{:S(2)}) async-start(), calls=%async_computation.6 | async-start | bytes 5308416 | tf_op jit(solution)/shard_map/reduce_scatter | solution.py:417
  252.5 1.1 copy-start.4
  252.6 176.0 %reduce-scatter.11.cloned.1.call-start = ((), (), s32[]{:S(2)}) async-start(), calls=%async_computation.7 | async-start | bytes 5308416 | tf_op jit(solution)/shard_map/reduce_scatter | solution.py:417
  260.4 0.7 copy-start.3
  260.4 1.4 copy-start.1
  260.4 2.4 copy-start.2
  278.8 151.9 %copy-start = (bf16[2,256,768]{2,1,0:T(8,128)(2,1)S(1)}, bf16[2,256,768]{2,1,0:T(8,128)(2,1)}, u32[]{:S(2)}) copy-start(bf16[2,256,768]{2,1,0:T(8,128)(2,1)} %get-tuple-element.19) | copy-start | bytes 2359300
Sparse Core Ops, SparseCore 0:
  239.6 32.7 reduce-scatter.6
  274.7 42.4 reduce-scatter.4
  319.6 53.3 reduce-scatter.8
  375.2 53.3 reduce-scatter.10

commit v2 on v1

v2 whole, which is shorter than its diff:
```python
import functools
import math
from types import SimpleNamespace

import jax
import jax.numpy as jnp
from jax import lax
from jax.experimental import pallas as pl
from jax.experimental.pallas import tpu as pltpu
from jax.sharding import PartitionSpec as P

HEADS = 12
TEMB = 128
SHORT = 128
TILE = 256
CHUNK = 32
CORES = 2
DEEP = 4
norm_eps = 1e-06
MESH = pl.DeviceIdType.MESH
low = jnp.bfloat16
wide = jnp.float32


def dot_nn(a, b):
    return lax.dot_general(a, b, (((1,), (0,)), ((), ())), preferred_element_type=wide)


def dot_nt(a, b):
    return lax.dot_general(a, b, (((1,), (1,)), ((), ())), preferred_element_type=wide)


def dot_tn(a, b):
    return lax.dot_general(a, b, (((0,), (0,)), ((), ())), preferred_element_type=wide)


def fold(block):
    total = block[0:8]
    for start in range(8, block.shape[0], 8):
        total = total + block[start : start + 8]
    return total


GELU_C = math.sqrt(2.0 / math.pi)


def gelu(u):
    t = jnp.tanh(GELU_C * (u + 0.044715 * (u * u * u)))
    return 0.5 * u * (1.0 + t)


def gelu_both(u):
    square = u * u
    t = jnp.tanh(GELU_C * (u + 0.044715 * (square * u)))
    outer = 0.5 * (1.0 + t)
    slope = outer + 0.5 * u * (1.0 - t * t) * (GELU_C * (1.0 + (3.0 * 0.044715) * square))
    return u * outer, slope


def chain_kernel(names, sections, fused, *refs):
    r = SimpleNamespace(**dict(zip(names, refs)))
    micro, rows, width = r.x.shape
    ff = r.win.shape[1]
    qkv_width = 3 * width
    half_rows = SHORT
    chunks = [(start, start // half_rows) for start in range(0, rows, CHUNK)]
    halves = rows // half_rows
    section = lax.axis_index("section")
    member = lax.axis_index("dp")
    z_at = lax.div(member, CORES)
    core = lax.rem(member, CORES)
    own = z_at if fused else 0
    right = lax.rem(section + 1, sections)
    left = lax.rem(section + sections - 1, sections)
    is_first = section == 0
    is_last = section == sections - 1

    loads = []
    for index, (hbm, vmem) in enumerate(
        (
            (r.wqkv_h, r.wa.at[:, 0:qkv_width]),
            (r.wout_h, r.wa.at[:, qkv_width:]),
            (r.win_h, r.win),
            (r.wdown_h, r.wdown),
        )
    ):
        loads.append(pltpu.make_async_copy(hbm, vmem, r.wsem.at[index]))
        loads[index].start()

    barrier = pltpu.get_barrier_semaphore()
    greeted = [(left, member), (right, member)]
    if fused:
        greeted.append((section, z_at * CORES + 1 - core))
        for away in range(1, DEEP):
            greeted.append((section, lax.rem(z_at + away, DEEP) * CORES + core))
    for target in greeted:
        pl.semaphore_signal(barrier, inc=1, device_id=target, device_id_type=MESH)
    pl.semaphore_wait(barrier, len(greeted))

    def remote(src, dst, send_sem, recv_sem, target):
        return pltpu.make_async_remote_copy(
            src_ref=src,
            dst_ref=dst,
            send_sem=send_sem,
            recv_sem=recv_sem,
            device_id=target,
            device_id_type=MESH,
        )

    def forward_copy(job, slot):
        return remote(
            r.fout.at[job], r.frecv.at[mb_rows(slot), :], r.fss.at[job], r.frs.at[slot], (right, member)
        )

    def backward_copy(job):
        return remote(
            r.gin.at[job], r.brecv.at[job], r.bss.at[job], r.brs.at[job], (left, member)
        )

    def mod_row(mb, half, k):
        return r.mod[mb, half, pl.ds(k, 1), :]

    def mb_rows(mb):
        return pl.ds(pl.multiple_of(mb * rows, rows), rows)

    def mb_span(mb, start):
        return pl.ds(pl.multiple_of(mb * rows + start, CHUNK), CHUNK)

    lane = lax.broadcasted_iota(jnp.int32, (1, 128), 1)
    first_lanes = lane < 64
    masks = [first_lanes.astype(wide).astype(low), (1.0 - first_lanes.astype(wide)).astype(low)]
    scale = (width // HEADS) ** (-0.5)

    near = (1, 2, -1, -2)

    def spread_copy(buffer, send_sems, recv_sems, mb, k):
        target = jnp.clip(z_at + near[k], 0, DEEP - 1)
        return remote(
            buffer.at[mb, z_at],
            buffer.at[mb, z_at],
            send_sems.at[mb, k],
            recv_sems.at[mb, z_at],
            (section, target * CORES + core),
        )

    def spread(buffer, send_sems, recv_sems, mb, wait):
        for k in range(len(near)):

            @pl.when(jnp.logical_and(z_at + near[k] >= 0, z_at + near[k] < DEEP))
            def _():
                copy = spread_copy(buffer, send_sems, recv_sems, mb, k)
                copy.wait_send() if wait else copy.start()

    def relay(buffer, send_sems, recv_sems, mb, wait):
        for at, source, target in ((2, 0, 3), (1, 3, 0)):

            @pl.when(z_at == at)
            def _():
                copy = remote(
                    buffer.at[mb, source],
                    buffer.at[mb, source],
                    send_sems.at[mb, len(near)],
                    recv_sems.at[mb, source],
                    (section, target * CORES + core),
                )
                if wait:
                    copy.wait_send()
                else:
                    copy.wait_recv()
                    copy.start()

    def await_block(buffer, send_sems, recv_sems, mb, source):
        relayed = jnp.logical_or(
            jnp.logical_and(z_at == 2, source == 0), jnp.logical_and(z_at == 1, source == 3)
        )

        @pl.when(jnp.logical_and(z_at != source, jnp.logical_not(relayed)))
        def _():
            remote(
                buffer.at[mb, source],
                buffer.at[mb, source],
                send_sems.at[mb, 0],
                recv_sems.at[mb, source],
                (section, member),
            ).wait_recv()

    def norm_forward(src, mb, k_shift, k_scale, n_keep, r_keep, out):
        for start, half in chunks:
            span = pl.ds(start, CHUNK)
            v = src[span, :]
            centered = v - jnp.mean(v, axis=-1, keepdims=True)
            inverse = lax.rsqrt(jnp.mean(centered * centered, axis=-1, keepdims=True) + norm_eps)
            n = centered * inverse
            n_keep[mb_span(mb, start), :] = n.astype(low)
            r_keep[mb, span, :] = inverse
            out[span, :] = (
                n * (1.0 + mod_row(mb, half, k_scale)) + mod_row(mb, half, k_shift)
            ).astype(low)

    r.dmod[...] = jnp.zeros_like(r.dmod)

    def forward_job(job, carry):
        mb = lax.rem(job, micro)
        here = mb_rows(mb)
        z_base = 0 if fused else mb * (ff // width)

        @pl.when(jnp.logical_or(jnp.logical_not(is_first), job >= micro))
        def _():
            forward_copy(job, job).wait_recv()

        @pl.when(jnp.logical_and(is_first, job < micro))
        def _():
            r.h[...] = r.x[mb].astype(wide)

        @pl.when(jnp.logical_and(is_first, job >= micro))
        def _():
            r.h[...] = r.x[mb].astype(wide) + r.frecv[mb_rows(job), :].astype(wide)

        @pl.when(jnp.logical_not(is_first))
        def _():
            r.h[...] = r.frecv[mb_rows(job), :].astype(wide)

        norm_forward(r.h, mb, 0, 1, r.n1, r.r1, r.a1.at[mb])

        def wait_load(index):
            @pl.when(job == 0)
            def _():
                loads[index].wait()

        wait_load(0)
        a1 = r.a1[mb]
        for c in range(0, 3 * width, TILE):
            r.qkvo[here, c : c + TILE] = dot_nn(a1, r.wa[:, c : c + TILE]).astype(low)
        bias = r.bias[mb]
        for c in range(0, width, 128):
            q, k, v = [r.qkvo[here, i * width + c : i * width + c + 128] for i in range(3)]
            outs = []
            for mask in masks:
                s = dot_nt(q * (mask * scale), k) + bias
                e = jnp.exp(s - jnp.max(s, axis=1, keepdims=True))
                p = (e * (1.0 / jnp.sum(e, axis=1, keepdims=True))).astype(low)
                outs.append(dot_nn(p, v))
            r.qkvo[here, qkv_width + c : qkv_width + c + 128] = jnp.where(
                first_lanes, outs[0], outs[1]
            ).astype(low)
        wait_load(1)
        o = r.qkvo[here, qkv_width:]
        for c in range(0, width, TILE):
            r.t[:, c : c + TILE] = dot_nn(o, r.wa[:, qkv_width + c : qkv_width + c + TILE])
        for start, half in chunks:
            span = pl.ds(start, CHUNK)
            attn = r.t[span, :]
            r.dattn[mb, span, :] = attn.astype(low)
            r.m[span, :] = r.h[span, :] + mod_row(mb, half, 2) * attn
        norm_forward(r.m, mb, 3, 4, r.n2, r.r2, r.a2.at[mb, own])
        if fused:

            @pl.when(job >= micro)
            def _():
                spread(r.a2, r.a2ss, r.a2rs, mb, False)

        wait_load(2)
        a2 = r.a2[mb, own]
        for c in range(0, ff, TILE):
            u = dot_nn(a2, r.win[:, c : c + TILE])
            r.du[mb_rows(mb), c : c + TILE] = u.astype(low)
            at = c % width
            r.z[z_base + c // width, :, at : at + TILE] = gelu(u).astype(low)
        wait_load(3)
        z = [r.z[z_base + i] for i in range(ff // width)]
        for c in range(0, width, TILE):
            y = dot_nn(z[0], r.wdown[0:width, c : c + TILE])
            for i in range(1, ff // width):
                y = y + dot_nn(z[i], r.wdown[i * width : (i + 1) * width, c : c + TILE])
            r.t[:, c : c + TILE] = y
        for start, half in chunks:
            span = pl.ds(start, CHUNK)
            y = r.t[span, :]
            r.y[mb, span, :] = y.astype(low)
            r.fout[job, span, :] = (r.m[span, :] + mod_row(mb, half, 5) * y).astype(low)

        @pl.when(jnp.logical_or(jnp.logical_not(is_last), job < micro))
        def _():
            forward_copy(job, jnp.where(is_last, job + micro, job)).start()

        return carry

    lax.fori_loop(0, 2 * micro, forward_job, 0)
    if fused:
        pl.semaphore_signal(
            r.done,
            inc=1,
            device_id=(section, z_at * CORES + 1 - core),
            device_id_type=MESH,
        )

    def norm_backward(mb, k_scale, n_keep, r_keep, base, per_chunk):
        for half in range(halves):
            shift_sum = jnp.zeros((8, width), wide)
            scale_sum = jnp.zeros((8, width), wide)
            gate_sum = jnp.zeros((8, width), wide)
            for start in range(half * half_rows, (half + 1) * half_rows, CHUNK):
                span = pl.ds(start, CHUNK)
                da = r.t[span, :]
                n = n_keep[mb_span(mb, start), :].astype(wide)
                inverse = r_keep[mb, span, :]
                shift_sum = shift_sum + fold(da)
                scale_sum = scale_sum + fold(da * n)
                dn = da * (1.0 + mod_row(mb, half, k_scale))
                dv = inverse * (
                    dn
                    - jnp.mean(dn, axis=-1, keepdims=True)
                    - n * jnp.mean(dn * n, axis=-1, keepdims=True)
                )
                extra = per_chunk(span, half, base[span, :] + dv)
                if extra is not None:
                    gate_sum = gate_sum + fold(extra)
            r.dmod[mb, half, k_scale - 1, :] = jnp.sum(shift_sum, axis=0)
            r.dmod[mb, half, k_scale, :] = jnp.sum(scale_sum, axis=0)
            if k_scale == 4:
                r.dmod[mb, half, 2, :] = jnp.sum(gate_sum, axis=0)

    def backward_job(mb, carry):
        g_s = r.h
        here = mb_rows(mb)

        @pl.when(is_last)
        def _():
            g_s[...] = r.cot[mb].astype(wide)

        @pl.when(jnp.logical_not(is_last))
        def _():
            backward_copy(mb).wait_recv()
            g_s[...] = r.brecv[mb].astype(wide)

        for half in range(halves):
            gate_sum = jnp.zeros((8, width), wide)
            for start in range(half * half_rows, (half + 1) * half_rows, CHUNK):
                span = pl.ds(start, CHUNK)
                g = g_s[span, :]
                gate_sum = gate_sum + fold(g * r.y[mb, span, :].astype(wide))
                r.dy[mb, own, span, :] = (mod_row(mb, half, 5) * g).astype(low)
            r.dmod[mb, half, 5, :] = jnp.sum(gate_sum, axis=0)
        if fused:
            spread(r.dy, r.dyss, r.dyrs, mb, False)
        dy = r.dy[mb, own]
        for c in range(0, ff, TILE):
            dz = dot_nt(dy, r.wdown[c : c + TILE, :])
            u = r.du[mb_rows(mb), c : c + TILE].astype(wide)
            r.du[mb_rows(mb), c : c + TILE] = (gelu_both(u)[1] * dz).astype(low)
        du = r.du[mb_rows(mb), :]
        for c in range(0, width, TILE):
            r.t[:, c : c + TILE] = dot_nt(du, r.win[c : c + TILE, :])

        def after_mlp(span, half, dm):
            r.m[span, :] = dm
            extra = dm * r.dattn[mb, span, :].astype(wide)
            r.dattn[mb, span, :] = (mod_row(mb, half, 2) * dm).astype(low)
            return extra

        norm_backward(mb, 4, r.n2, r.r2, g_s, after_mlp)
        dattn = r.dattn[mb]
        for c in range(0, width, TILE):
            r.do[:, c : c + TILE] = dot_nt(dattn, r.wa[c : c + TILE, qkv_width:]).astype(low)
        bias = r.bias[mb]
        for c in range(0, width, 128):
            cols = [slice(i * width + c, i * width + c + 128) for i in range(3)]
            q, k, v = [r.qkvo[here, cut] for cut in cols]
            do = r.do[:, c : c + 128]
            parts = []
            for mask in masks:
                s = dot_nt(k, q * (mask * scale)) + bias
                e = jnp.exp(s - jnp.max(s, axis=0, keepdims=True))
                p = e * (1.0 / jnp.sum(e, axis=0, keepdims=True))
                dp = dot_nt(v * mask, do)
                inner = jnp.sum(p * dp, axis=0, keepdims=True)
                ds = (p * (dp - inner) * scale).astype(low)
                parts.append((dot_tn(ds, k), dot_nn(ds, q), dot_nn(p.astype(low), do)))
            for i in range(3):
                r.qkvo[here, cols[i]] = jnp.where(first_lanes, parts[0][i], parts[1][i]).astype(
                    low
                )
        dqkv = r.qkvo[here, 0:qkv_width]
        for c in range(0, width, TILE):
            r.t[:, c : c + TILE] = dot_nt(dqkv, r.wa[c : c + TILE, 0:qkv_width])

        def after_attention(span, half, dh):
            r.gin[mb, span, :] = dh.astype(low)

        norm_backward(mb, 1, r.n1, r.r1, r.m, after_attention)

        @pl.when(jnp.logical_not(is_first))
        def _():
            backward_copy(mb).start()

        return carry

    lax.fori_loop(0, micro, backward_job, 0)

    if fused:
        gradient_tail(r, section, z_at, core, member, remote, spread, relay, await_block)

    for job in range(2 * micro):

        @pl.when(jnp.logical_or(jnp.logical_not(is_last), job < micro))
        def _():
            forward_copy(job, job).wait_send()

    for job in range(micro):

        @pl.when(jnp.logical_not(is_first))
        def _():
            backward_copy(job).wait_send()


def gradient_tail(r, section, z_at, core, member, remote, spread, relay, await_block):
    micro, rows, width = r.x.shape
    ff = r.win.shape[1]
    share = width // (DEEP * CORES)
    part = ff // DEEP
    half_part = part // CORES
    other = 1 - core
    partner = (section, z_at * CORES + other)
    qkv_width = 3 * width

    def on_z(z):
        return (section, z * CORES + core)

    for step in (1, -1):

        @pl.when(jnp.logical_and(z_at + step >= 0, z_at + step < DEEP))
        def _():
            pl.semaphore_signal(
                r.free,
                inc=1,
                device_id=on_z(jnp.clip(z_at + step, 0, DEEP - 1)),
                device_id_type=MESH,
            )

    mine = r.ada.at[core, z_at]
    for mb in range(micro):
        sums = r.dmod[mb]
        mine[mb, :, 0:width] = sums.reshape(sums.shape[0] * sums.shape[1], width).astype(low)
        mine[mb, :, width:] = r.feat[mb]

    def ada_copy(away):
        target = lax.rem(z_at + away, DEEP)
        return remote(
            mine, mine, r.adass.at[away - 1], r.adars.at[z_at], (section, target * CORES + core)
        )

    for away in range(1, DEEP):
        ada_copy(away).start()

    def flat(ref):
        block = ref[...]
        return block.reshape(micro * rows, block.shape[-1])

    a1_t = flat(r.a1).T
    for c in range(0, qkv_width, TILE):
        r.wa[:, c : c + TILE] = dot_nn(a1_t, r.qkvo[:, c : c + TILE]).astype(low)
    o_t = r.qkvo[:, qkv_width:].T
    dattn = flat(r.dattn)
    for c in range(0, width, TILE):
        r.wa[:, qkv_width + c : qkv_width + c + TILE] = dot_nn(
            o_t, dattn[:, c : c + TILE]
        ).astype(low)

    def share_rows(z, of_core):
        return pl.ds(pl.multiple_of((z * CORES + of_core) * share, share), share)

    def pair_copy(z):
        return remote(
            r.wa.at[share_rows(z, other), :], r.pa.at[z], r.pss.at[z], r.prs.at[z], partner
        )

    for z in range(DEEP):
        pair_copy(z).start()

    for mb in range(micro):
        relay(r.a2, r.a2ss, r.a2rs, mb, False)
    relay(r.dy, r.dyss, r.dyrs, 0, False)

    group = 2

    def mlp_group(mb, first):
        for step in range(group):
            await_block(r.a2, r.a2ss, r.a2rs, mb, first + step)
            await_block(r.dy, r.dyss, r.dyrs, mb, first + step)
        tokens = group * rows
        a2 = r.a2[mb, pl.ds(first, group)].reshape(tokens, width)
        dy = r.dy[mb, pl.ds(first, group)].reshape(tokens, width)
        for c in range(0, part, TILE):
            at = pl.ds(pl.multiple_of(z_at * part + c, TILE), TILE)
            u = dot_nn(a2, r.win[:, at])
            dz = dot_nt(dy, r.wdown[at, :])
            active, slope = gelu_both(u)
            r.z[0:group, :, c : c + TILE] = active.astype(low).reshape(group, rows, TILE)
            r.z[group:, :, c : c + TILE] = (slope * dz).astype(low).reshape(group, rows, TILE)
        z_t = r.z[0:group].reshape(tokens, part).T
        a2_t = a2.T
        for c in range(0, width, TILE):
            r.pdown[:, c : c + TILE] += dot_nn(z_t, dy[:, c : c + TILE])
        for c in range(0, part, TILE):
            r.pin[:, c : c + TILE] += dot_nn(a2_t, r.z[group:, :, c : c + TILE].reshape(tokens, TILE))

    def sums(z):
        return r.qkvo.at[z * share : (z + 1) * share, :]

    def sum_pair():
        for z in range(DEEP):
            pair_copy(z).wait_recv()
            sums(z)[...] = (
                r.wa[share_rows(z, core), :].astype(wide) + r.pa[z].astype(wide)
            ).astype(low)

    def slot_of(z, direction):
        if direction > 0:
            return z - 1
        return DEEP - 1 + z if z < DEEP - 2 else 0

    def slot_ref(z, direction):
        return r.du.at[pl.ds(slot_of(z, direction) * share, share), :]

    def line_copy(z, direction):
        slot = slot_of(z, direction)
        return remote(
            sums(z),
            slot_ref(z, direction),
            r.lss.at[z],
            r.lrs.at[slot],
            on_z(jnp.clip(z_at + direction, 0, DEEP - 1)),
        )

    def passes(z, direction):
        return z_at < z if direction > 0 else z_at > z

    def takes(direction):
        return z_at > 0 if direction > 0 else z_at < DEEP - 1

    def add_slot(z, direction):
        line_copy(z, direction).wait_recv()
        sums(z)[...] = (
            sums(z)[...].astype(wide) + slot_ref(z, direction)[...].astype(wide)
        ).astype(low)

    def line_start(z, direction):
        @pl.when(jnp.logical_and(passes(z, direction), jnp.logical_not(takes(direction))))
        def _():
            line_copy(z, direction).start()

    def line_pass(z, direction, at):
        @pl.when(z_at == at)
        def _():
            add_slot(z, direction)
            line_copy(z, direction).start()

    def group_step(g, carry):
        @pl.when(g == 0)
        def _():
            r.pdown[...] = jnp.zeros_like(r.pdown)
            r.pin[...] = jnp.zeros_like(r.pin)

        @pl.when(g == 2)
        def _():
            sum_pair()
            for at in range(DEEP):

                @pl.when(z_at == at)
                def _():
                    pl.semaphore_wait(r.free, (at > 0) + (at < DEEP - 1))

            for z in (3, 2, 1):
                line_start(z, 1)
                line_start(DEEP - 1 - z, -1)
            relay(r.dy, r.dyss, r.dyrs, 1, False)

        mlp_group(lax.div(g, 2), lax.rem(g, 2) * group)

        @pl.when(g == 2)
        def _():
            line_pass(3, 1, 1)
            line_pass(0, -1, 2)

        @pl.when(g == 3)
        def _():
            line_pass(2, 1, 1)
            line_pass(1, -1, 2)

        return carry

    lax.fori_loop(0, micro * DEEP // group, group_step, 0)

    def down_copy():
        return remote(
            r.n1.at[pl.ds(0, half_part), :],
            r.frecv.at[pl.ds(width // CORES, half_part), :],
            r.mss.at[DEEP],
            r.mrs.at[DEEP],
            partner,
        )

    def up_copy(z):
        return remote(
            r.cols.at[z],
            r.frecv.at[pl.ds(z * share, share), :],
            r.mss.at[z],
            r.mrs.at[z],
            partner,
        )

    pl.semaphore_wait(r.done, 1)
    for z in range(DEEP):
        r.cols[z] = r.pin[share_rows(z, other), :].astype(low)
        up_copy(z).start()
    r.n1[0:half_part, :] = r.pdown[
        pl.ds(pl.multiple_of(other * half_part, half_part), half_part), :
    ].astype(low)
    down_copy().start()

    def column_copy(z):
        return remote(
            r.cols2.at[z], r.land.at[z_at], r.css.at[z], r.crs.at[z_at], on_z(z)
        )

    def part_columns(z):
        return pl.ds(pl.multiple_of(z * part, part), part)

    for z in range(DEEP):
        up_copy(z).wait_recv()
        total = r.pin[share_rows(z, core), :] + r.frecv[z * share : (z + 1) * share, :].astype(wide)

        @pl.when(z_at == z)
        def _():
            r.g_up[:, part_columns(z)] = total

        @pl.when(z_at != z)
        def _():
            r.cols2[z] = total.astype(low)
            column_copy(z).start()

    line_pass(3, 1, 2)
    line_pass(0, -1, 1)

    def ada_pair():
        return remote(
            r.ada.at[core], r.ada.at[core], r.adass.at[DEEP - 1], r.adars.at[DEEP], partner
        )

    def ada_other():
        return remote(
            r.ada.at[other], r.ada.at[other], r.adass.at[DEEP - 1], r.adars.at[DEEP], partner
        )

    for z in range(DEEP):

        @pl.when(z_at != z)
        def _():
            remote(
                r.ada.at[core, z], r.ada.at[core, z], r.adass.at[0], r.adars.at[z], partner
            ).wait_recv()

    ada_pair().start()

    down_copy().wait_recv()
    own_half = pl.ds(pl.multiple_of(core * half_part, half_part), half_part)
    r.g_down[...] = r.pdown[own_half, :] + r.frecv[
        width // CORES : width // CORES + half_part, :
    ].astype(wide)

    ada_other().wait_recv()
    entries = CORES * DEEP * micro * r.feat.shape[1]
    ada_rows = TEMB // (DEEP * CORES)
    pick = lax.broadcasted_iota(jnp.int32, (ada_rows, TEMB), 1) == (
        lax.broadcasted_iota(jnp.int32, (ada_rows, TEMB), 0) + member * ada_rows
    )
    features = r.ada[:, :, :, :, width:].reshape(entries, TEMB)
    gathered = r.ada[:, :, :, :, 0:width].reshape(entries, width)
    spreads = dot_nt(pick.astype(wide).astype(low), features)
    which = lax.rem(lax.broadcasted_iota(jnp.int32, (ada_rows, entries), 1), 8)
    for k in range(6):
        chosen = jnp.where(which == k, spreads, 0.0).astype(low)
        r.g_ada[:, k * width : (k + 1) * width] = dot_nn(chosen, gathered)

    def finish(z):
        for direction in (1, -1):

            @pl.when(takes(direction))
            def _():
                if (direction > 0 and z > 0) or (direction < 0 and z < DEEP - 1):
                    line_copy(z, direction).wait_recv()
        total = sums(z)[...].astype(wide)
        if z > 0:
            total = total + slot_ref(z, 1)[...].astype(wide)
        if z < DEEP - 1:
            total = total + slot_ref(z, -1)[...].astype(wide)
        r.g_qkv[...] = total[:, 0:qkv_width]
        r.g_out[...] = total[:, qkv_width:]

    for z in range(DEEP):

        @pl.when(z_at == z)
        def _():
            finish(z)

    for z in range(DEEP):

        @pl.when(z_at != z)
        def _():
            remote(
                r.cols2.at[z], r.land.at[z], r.css.at[z], r.crs.at[z], on_z(z)
            ).wait_recv()
            r.g_up[:, z * part : (z + 1) * part] = r.land[z].astype(wide)

    for mb in range(micro):
        spread(r.a2, r.a2ss, r.a2rs, mb, True)
        spread(r.dy, r.dyss, r.dyrs, mb, True)
        relay(r.a2, r.a2ss, r.a2rs, mb, True)
        relay(r.dy, r.dyss, r.dyrs, mb, True)
    for away in range(1, DEEP):
        ada_copy(away).wait_send()
    ada_pair().wait_send()
    for z in range(DEEP):
        pair_copy(z).wait_send()
        up_copy(z).wait_send()

        @pl.when(z_at != z)
        def _():
            column_copy(z).wait_send()
            line_copy(z, 1 if z > 0 else -1).wait_send()

    down_copy().wait_send()


def run_chain(x, cot, mod, bias, feat, w_qkv, w_out, w_in, w_down, members):
    micro, rows, width = x.shape
    ff = w_in.shape[1]
    sections = lax.axis_size("section")
    fused = members == DEEP * CORES
    vmem = pl.BlockSpec(memory_space=pltpu.VMEM)
    hbm = pl.BlockSpec(memory_space=pl.ANY)
    dma = pltpu.SemaphoreType.DMA

    def kept(*shape):
        return jax.ShapeDtypeStruct(shape, low)

    def result(*shape):
        return jax.ShapeDtypeStruct(shape, wide)

    names = ["x", "cot", "mod", "bias", "feat", "wqkv_h", "wout_h", "win_h", "wdown_h"]
    in_specs = [vmem] * 5 + [hbm] * 4
    stored = {
        "dmod": result(*mod.shape),
        "a1": kept(micro, rows, width),
        "qkvo": kept(micro * rows, 4 * width),
        "dattn": kept(micro, rows, width),
        "a2": kept(micro, DEEP if fused else 1, rows, width),
        "du": kept(micro * rows, ff),
        "z": kept((1 if fused else micro) * (ff // width), rows, width),
        "dy": kept(micro, DEEP if fused else 1, rows, width),
    }
    outs = {"fout": kept(2 * micro, rows, width), "gin": kept(micro, rows, width)}
    share = width // members
    if fused:
        outs["g_qkv"] = result(share, 3 * width)
        outs["g_out"] = result(share, width)
        outs["g_up"] = result(share, ff)
        outs["g_down"] = result(ff // members, width)
        outs["g_ada"] = result(TEMB // members, 6 * width)
    else:
        outs.update(stored)
    scratch = {
        "wa": pltpu.VMEM((width, 4 * width), low),
        "win": pltpu.VMEM((width, ff), low),
        "wdown": pltpu.VMEM((ff, width), low),
        "h": pltpu.VMEM((rows, width), wide),
        "m": pltpu.VMEM((rows, width), wide),
        "t": pltpu.VMEM((rows, width), wide),
        "do": pltpu.VMEM((rows, width), low),
        "n1": pltpu.VMEM((micro * rows, width), low),
        "n2": pltpu.VMEM((micro * rows, width), low),
        "r1": pltpu.VMEM((micro, rows, 1), wide),
        "r2": pltpu.VMEM((micro, rows, 1), wide),
        "y": pltpu.VMEM((micro, rows, width), low),
        "frecv": pltpu.VMEM((2 * micro * rows, width), low),
        "brecv": pltpu.VMEM((micro, rows, width), low),
        "wsem": dma((4,)),
        "fss": dma((2 * micro,)),
        "frs": dma((2 * micro,)),
        "bss": dma((micro,)),
        "brs": dma((micro,)),
    }
    if fused:
        part = ff // DEEP
        for name, value in stored.items():
            scratch[name] = pltpu.VMEM(value.shape, value.dtype)
        scratch.update(
            {
                "pa": pltpu.VMEM((DEEP, share, 4 * width), low),
                "pdown": pltpu.VMEM((part, width), wide),
                "pin": pltpu.VMEM((width, part), wide),
                "cols": pltpu.VMEM((DEEP, share, part), low),
                "cols2": pltpu.VMEM((DEEP, share, part), low),
                "land": pltpu.VMEM((DEEP, share, part), low),
                "ada": pltpu.VMEM((CORES, DEEP, micro, feat.shape[1], width + TEMB), low),
                "free": pltpu.SemaphoreType.REGULAR,
                "done": pltpu.SemaphoreType.REGULAR,
                "a2ss": dma((micro, 5)),
                "a2rs": dma((micro, DEEP)),
                "dyss": dma((micro, 5)),
                "dyrs": dma((micro, DEEP)),
                "adass": dma((DEEP,)),
                "adars": dma((DEEP + 1,)),
                "pss": dma((DEEP,)),
                "prs": dma((DEEP,)),
                "lss": dma((DEEP,)),
                "lrs": dma((5,)),
                "mss": dma((DEEP + 1,)),
                "mrs": dma((DEEP + 1,)),
                "css": dma((DEEP,)),
                "crs": dma((DEEP,)),
            }
        )
    names = names + list(outs) + list(scratch)
    values = pl.pallas_call(
        functools.partial(chain_kernel, names, sections, fused),
        out_shape=tuple(outs.values()),
        in_specs=in_specs,
        out_specs=(vmem,) * len(outs),
        scratch_shapes=list(scratch.values()),
        compiler_params=pltpu.CompilerParams(
            collective_id=0, has_side_effects=True, vmem_limit_bytes=60 * 1024 * 1024
        ),
    )(x, cot, mod, bias, feat, w_qkv, w_out, w_in, w_down)
    return SimpleNamespace(**dict(zip(outs, values)))


def time_features(timestep_ids):
    half_width = TEMB // 2
    frequency = jnp.exp(-math.log(10000.0) * jnp.arange(half_width, dtype=wide) / half_width)
    angles = timestep_ids.astype(wide)[:, None] * 0.1 * frequency[None, :]
    return jnp.concatenate([jnp.sin(angles), jnp.cos(angles)], axis=1)


def summed_apart(kept, features, micro, rows, width):
    def product(left, right):
        left = left.reshape(micro * rows, -1)
        right = right.reshape(micro * rows, -1)
        partial = dot_tn(left, right).astype(low)
        return lax.psum_scatter(partial, "dp", scatter_dimension=0, tiled=True).astype(wide)

    sums = kept.dmod[:, :, :6].reshape(features.shape[0], 6 * width)
    features_all = lax.all_gather(features.astype(wide), "dp", tiled=True)
    sums_all = lax.all_gather(sums, "dp", tiled=True)
    share = TEMB // lax.axis_size("dp")
    mine = lax.dynamic_slice_in_dim(features_all, lax.axis_index("dp") * share, share, 1)
    grad_ada = lax.dot_general(
        mine, sums_all, (((0,), (0,)), ((), ())), precision=lax.Precision.HIGHEST
    )
    return (
        product(kept.a1, kept.qkvo[:, : 3 * width]),
        product(kept.qkvo[:, 3 * width :], kept.dattn),
        product(kept.a2, kept.du),
        product(jnp.swapaxes(kept.z.reshape(micro, -1, rows, width), 1, 2), kept.dy),
        grad_ada,
    )


def on_device(inputs, cotangent, long_count, timesteps, w_qkv, w_out, w_in, w_down, ada_weight):
    micro = long_count.shape[1]
    width = inputs.shape[1]
    rows = inputs.shape[0] // micro
    halves = rows // SHORT
    members = lax.axis_size("dp")
    is_long = (long_count[0] == 1)[:, None]
    half_index = jnp.arange(halves, dtype=jnp.int32)[None, :]
    half_steps = jnp.where(is_long, timesteps[0][:, :1], timesteps[0][:, :halves])
    features = time_features(half_steps.reshape(-1)).astype(low)
    mod = jnp.dot(features, ada_weight[0], preferred_element_type=wide)
    mod = mod.reshape(micro, halves, 6, width)
    mod = jnp.pad(mod, ((0, 0), (0, 0), (0, 2), (0, 0)))
    feat = jnp.repeat(features.reshape(micro, halves, TEMB), 8, axis=1)
    slot_ids = jnp.where(is_long, 0, jnp.repeat(half_index, SHORT, axis=1))
    same = slot_ids[:, :, None] == slot_ids[:, None, :]
    bias = jnp.where(same, 0.0, -1e30).astype(wide)
    kept = run_chain(
        inputs.reshape(micro, rows, width),
        cotangent.reshape(micro, rows, width),
        mod,
        bias,
        feat,
        w_qkv[0],
        w_out[0],
        w_in[0],
        w_down[0],
        members,
    )
    if members == DEEP * CORES:
        grads = (kept.g_qkv, kept.g_out, kept.g_up, kept.g_down, kept.g_ada)
    else:
        grads = summed_apart(kept, features, micro, rows, width)
    hidden_out = kept.fout[micro:].reshape(1, micro * rows, width)
    grad_in = kept.gin.reshape(1, micro * rows, width)
    return (hidden_out, grad_in) + tuple(grad[None] for grad in grads)


def solution(mesh):
    placed = (
        P("dp", None),
        P("dp", None),
        P("dp", None),
        P("dp", None, None),
        P("section", None, None),
        P("section", None, None),
        P("section", None, None),
        P("section", None, None),
        P("section", None, None),
    )
    return jax.shard_map(
        on_device,
        mesh=mesh,
        in_specs=placed,
        out_specs=(P("section", "dp", None),) * 7,
        check_vma=False,
    )
```

time: 439 us -> 339 us (0.77)
  waiting for transfers between devices: 129 us -> 0 us
  Pallas kernels: 223 us -> 321 us
  blocking collectives: 29.3 us -> 0 us
  matrix products: 23.3 us -> 0.41 us
  between operations: 13.9 us -> 0.69 us
  other arithmetic: 10.7 us -> 2.63 us
    reduce_scatter x4 -> x0, waiting for transfers between devices: 129 us -> none  [product(): lax.psum_scatter(partial, 'dp', scatter_dimension=0, tiled=True)]
    pallas_call x1, Pallas kernels: 223 us -> 321 us  [run_chain(): pl.pallas_call(functools.partial(chain_kernel, names, sections, fused), o...]
    all_gather x2 -> x0, blocking collectives: 29.3 us -> none  [the longest x1 15.8 us: on_device(): lax.all_gather(dmod[:, :, :6].reshape(micro * halves, 6 * width), 'dp', t...]
    dot_general x5 -> x0, matrix products: 22.9 us -> none  [the longest x4 21.6 us: dot_tn(): lax.dot_general(a, b, (((0,), (0,)), ((), ())), preferred_element_type=wide)]
    broadcast_in_dim x4 -> x0, other arithmetic: 7.95 us -> none  [the longest x1 2.18 us: on_device(): grad_up[None]]
  transfers between devices with their start and end apart: 4 -> 0, of which waited for: 3 -> 0; matrix products, arithmetic and copies ran while one was open for 6% -> 0% of each run, Pallas kernels for 0% -> 0%
where the time goes in v2:
time: 339 us; the launch traced here: 337 us
  Pallas kernels  321 us (95%)
  local copies, waits for them, and re-layouts  12.7 us (4%)
    pallas_call x1, Pallas kernels, run_chain(): pl.pallas_call(functools.partial(chain_kernel, names, sections, fused), o...  321 us
    unnamed x19, local copies, waits for them, and re-layouts  8.52 us

profile of v2, /device:TPU:0, one launch (start us, length us, event | category | flops | bytes accessed | tf_op | source)
XLA Modules:
  0.0 337.4 jit_solution(15420521152366913290)
XLA Ops:
  0.6 0.7 compare_bitcast_fusion
  1.3 0.8 slice_reduce_fusion
  2.1 0.8 convert_multiply_fusion
  2.8 0.1 fusion
  3.0 0.1 pad_maximum_fusion
  3.1 0.1 broadcast_select_fusion
  3.1 0.6 broadcast_bitcast_fusion.refs_4_
  3.7 0.9 compare_select_fusion.refs_3_
  4.7 1.7 copy.18
  6.4 0.4 fusion.2
  6.8 0.7 pad.4.refs_2_
  7.5 320.9 %shard_map.144 = (bf16[4,256,768]{2,1,0:T(8,128)(2,1)}, bf16[2,256,768]{2,1,0:T(8,128)(2,1)}, f32[96,2304]{1,0:T(8,128)}, f32[96,768]{1,0:T(8,128)}, f32[96,3072...) custom-call(bf16[2,256,768]{2,1,0:T(8,128)(2,1)} %bitcast.42, bf16[2,256,768]{2,1,0:T(8,128)(2,1)} %bitcast.43, ...), custom_call_target="tpu_custom_call" | custom-call | tf_op jit(solution)/shard_map/pallas_call | solution.py:825
  328.4 0.0 copy-start.3
  328.4 2.1 slice.7
  330.6 0.9 copy.27
  331.4 0.6 copy-done.2
  332.0 0.9 copy.28
  332.9 0.2 copy-done.5
  333.1 0.7 copy.29
  333.9 1.0 copy.30
  334.9 0.7 copy-done
  335.6 1.0 copy.31
  336.6 0.1 copy-done.4
  336.7 0.7 copy.32
  (10 shorter events, 0.1 us)
Async XLA Ops:
  328.4 2.2 copy-start.3
  330.6 1.5 copy-start.2
  332.0 1.1 copy-start.5
  332.0 1.8 copy-start.1
  333.9 1.7 copy-start
  335.5 1.1 copy-start.4

commit v3 on v2

--- a/solution.py
+++ b/solution.py
@@ -63,7 +63,10 @@
     ff = r.win.shape[1]
     qkv_width = 3 * width
     half_rows = SHORT
-    chunks = [(start, start // half_rows) for start in range(0, rows, CHUNK)]
+
+    def half_chunks(half):
+        return range(half * half_rows, (half + 1) * half_rows, CHUNK)
+
     halves = rows // half_rows
     section = lax.axis_index("section")
     member = lax.axis_index("dp")
@@ -107,14 +110,27 @@
             device_id_type=MESH,
         )
 
-    def forward_copy(job, slot):
-        return remote(
-            r.fout.at[job], r.frecv.at[mb_rows(slot), :], r.fss.at[job], r.frs.at[slot], (right, member)
-        )
-
-    def backward_copy(job):
-        return remote(
-            r.gin.at[job], r.brecv.at[job], r.bss.at[job], r.brs.at[job], (left, member)
+    def forward_copy(job, slot, half):
+        span = pl.ds(half * half_rows, half_rows)
+        landing = pl.ds(
+            pl.multiple_of(slot * rows + half * half_rows, half_rows), half_rows
+        )
+        return remote(
+            r.fout.at[job, span, :],
+            r.frecv.at[landing, :],
+            r.fss.at[job, half],
+            r.frs.at[slot, half],
+            (right, member),
+        )
+
+    def backward_copy(job, half):
+        span = pl.ds(half * half_rows, half_rows)
+        return remote(
+            r.gin.at[job, span, :],
+            r.brecv.at[job, span, :],
+            r.bss.at[job, half],
+            r.brs.at[job, half],
+            (left, member),
         )
 
     def mod_row(mb, half, k):
@@ -130,6 +146,7 @@
     first_lanes = lane < 64
     masks = [first_lanes.astype(wide).astype(low), (1.0 - first_lanes.astype(wide)).astype(low)]
     scale = (width // HEADS) ** (-0.5)
+    ones = jnp.ones((rows, 128), low)
 
     near = (1, 2, -1, -2)
 
@@ -184,8 +201,8 @@
                 (section, member),
             ).wait_recv()
 
-    def norm_forward(src, mb, k_shift, k_scale, n_keep, r_keep, out):
-        for start, half in chunks:
+    def norm_forward(src, mb, half, k_shift, k_scale, n_keep, r_keep, out):
+        for start in half_chunks(half):
             span = pl.ds(start, CHUNK)
             v = src[span, :]
             centered = v - jnp.mean(v, axis=-1, keepdims=True)
@@ -204,84 +221,109 @@
         here = mb_rows(mb)
         z_base = 0 if fused else mb * (ff // width)
 
-        @pl.when(jnp.logical_or(jnp.logical_not(is_first), job >= micro))
-        def _():
-            forward_copy(job, job).wait_recv()
-
-        @pl.when(jnp.logical_and(is_first, job < micro))
-        def _():
-            r.h[...] = r.x[mb].astype(wide)
-
-        @pl.when(jnp.logical_and(is_first, job >= micro))
-        def _():
-            r.h[...] = r.x[mb].astype(wide) + r.frecv[mb_rows(job), :].astype(wide)
-
-        @pl.when(jnp.logical_not(is_first))
-        def _():
-            r.h[...] = r.frecv[mb_rows(job), :].astype(wide)
-
-        norm_forward(r.h, mb, 0, 1, r.n1, r.r1, r.a1.at[mb])
-
         def wait_load(index):
             @pl.when(job == 0)
             def _():
                 loads[index].wait()
 
-        wait_load(0)
-        a1 = r.a1[mb]
-        for c in range(0, 3 * width, TILE):
-            r.qkvo[here, c : c + TILE] = dot_nn(a1, r.wa[:, c : c + TILE]).astype(low)
-        bias = r.bias[mb]
+        for half in range(halves):
+            span = pl.ds(half * half_rows, half_rows)
+            arrived = pl.ds(
+                pl.multiple_of(job * rows + half * half_rows, half_rows), half_rows
+            )
+
+            @pl.when(jnp.logical_or(jnp.logical_not(is_first), job >= micro))
+            def _():
+                forward_copy(job, job, half).wait_recv()
+
+            @pl.when(jnp.logical_and(is_first, job < micro))
+            def _():
+                r.h[span, :] = r.x[mb, span, :].astype(wide)
+
+            @pl.when(jnp.logical_and(is_first, job >= micro))
+            def _():
+                r.h[span, :] = r.x[mb, span, :].astype(wide) + r.frecv[arrived, :].astype(wide)
+
+            @pl.when(jnp.logical_not(is_first))
+            def _():
+                r.h[span, :] = r.frecv[arrived, :].astype(wide)
+
+            norm_forward(r.h, mb, half, 0, 1, r.n1, r.r1, r.a1.at[mb])
+            if half == 0:
+                wait_load(0)
+            a1 = r.a1[mb, span, :]
+            to = pl.ds(pl.multiple_of(mb * rows + half * half_rows, half_rows), half_rows)
+            for c in range(0, qkv_width, TILE):
+                r.qkvo[to, c : c + TILE] = dot_nn(a1, r.wa[:, c : c + TILE]).astype(low)
+
+        q_tag = r.tags[0, mb]
+        k_tag = r.tags[1, mb]
+
+        def scores(c):
+            q, k, v = [r.qkvo[here, i * width + c : i * width + c + 128] for i in range(3)]
+            k_wide = jnp.concatenate([k, k_tag], axis=1)
+            found = [
+                dot_nt(jnp.concatenate([q * (mask * scale), q_tag], axis=1), k_wide)
+                for mask in masks
+            ]
+            return found, jnp.concatenate([v, ones], axis=1)
+
+        def mix(c, found, v_wide):
+            weights = [jnp.exp(s - jnp.max(s, axis=1, keepdims=True)).astype(low) for s in found]
+            mixed = [dot_nn(e, v_wide) for e in weights]
+            top = jnp.where(first_lanes, mixed[0][:, 0:128], mixed[1][:, 0:128])
+            total = jnp.where(first_lanes, mixed[0][:, 128:], mixed[1][:, 128:])
+            r.do[:, c : c + 128] = (top * (1.0 / total)).astype(low)
+
+        ahead = scores(0)
         for c in range(0, width, 128):
-            q, k, v = [r.qkvo[here, i * width + c : i * width + c + 128] for i in range(3)]
-            outs = []
-            for mask in masks:
-                s = dot_nt(q * (mask * scale), k) + bias
-                e = jnp.exp(s - jnp.max(s, axis=1, keepdims=True))
-                p = (e * (1.0 / jnp.sum(e, axis=1, keepdims=True))).astype(low)
-                outs.append(dot_nn(p, v))
-            r.qkvo[here, qkv_width + c : qkv_width + c + 128] = jnp.where(
-                first_lanes, outs[0], outs[1]
-            ).astype(low)
+            current = ahead
+            if c + 128 < width:
+                ahead = scores(c + 128)
+            mix(c, *current)
         wait_load(1)
-        o = r.qkvo[here, qkv_width:]
-        for c in range(0, width, TILE):
-            r.t[:, c : c + TILE] = dot_nn(o, r.wa[:, qkv_width + c : qkv_width + c + TILE])
-        for start, half in chunks:
-            span = pl.ds(start, CHUNK)
-            attn = r.t[span, :]
-            r.dattn[mb, span, :] = attn.astype(low)
-            r.m[span, :] = r.h[span, :] + mod_row(mb, half, 2) * attn
-        norm_forward(r.m, mb, 3, 4, r.n2, r.r2, r.a2.at[mb, own])
+        wait_load(2)
+        wait_load(3)
+        r.qkvo[here, qkv_width:] = r.do[...]
+        for half in range(halves):
+            span = pl.ds(half * half_rows, half_rows)
+            to = pl.ds(pl.multiple_of(mb * rows + half * half_rows, half_rows), half_rows)
+            o = r.do[span, :]
+            for c in range(0, width, TILE):
+                r.t[span, c : c + TILE] = dot_nn(o, r.wa[:, qkv_width + c : qkv_width + c + TILE])
+            for start in half_chunks(half):
+                part = pl.ds(start, CHUNK)
+                attn = r.t[part, :]
+                r.dattn[mb, part, :] = attn.astype(low)
+                r.m[part, :] = r.h[part, :] + mod_row(mb, half, 2) * attn
+            norm_forward(r.m, mb, half, 3, 4, r.n2, r.r2, r.a2.at[mb, own])
+            a2 = r.a2[mb, own, span, :]
+            for c in range(0, ff, TILE):
+                u = dot_nn(a2, r.win[:, c : c + TILE])
+                r.du[to, c : c + TILE] = u.astype(low)
+                at = c % width
+                r.z[z_base + c // width, span, at : at + TILE] = gelu(u).astype(low)
+            z = [r.z[z_base + i, span, :] for i in range(ff // width)]
+            for c in range(0, width, TILE):
+                y = dot_nn(z[0], r.wdown[0:width, c : c + TILE])
+                for i in range(1, ff // width):
+                    y = y + dot_nn(z[i], r.wdown[i * width : (i + 1) * width, c : c + TILE])
+                r.t[span, c : c + TILE] = y
+            for start in half_chunks(half):
+                part = pl.ds(start, CHUNK)
+                y = r.t[part, :]
+                r.y[mb, part, :] = y.astype(low)
+                r.fout[job, part, :] = (r.m[part, :] + mod_row(mb, half, 5) * y).astype(low)
+
+            @pl.when(jnp.logical_or(jnp.logical_not(is_last), job < micro))
+            def _():
+                forward_copy(job, jnp.where(is_last, job + micro, job), half).start()
+
         if fused:
 
             @pl.when(job >= micro)
             def _():
                 spread(r.a2, r.a2ss, r.a2rs, mb, False)
-
-        wait_load(2)
-        a2 = r.a2[mb, own]
-        for c in range(0, ff, TILE):
-            u = dot_nn(a2, r.win[:, c : c + TILE])
-            r.du[mb_rows(mb), c : c + TILE] = u.astype(low)
-            at = c % width
-            r.z[z_base + c // width, :, at : at + TILE] = gelu(u).astype(low)
-        wait_load(3)
-        z = [r.z[z_base + i] for i in range(ff // width)]
-        for c in range(0, width, TILE):
-            y = dot_nn(z[0], r.wdown[0:width, c : c + TILE])
-            for i in range(1, ff // width):
-                y = y + dot_nn(z[i], r.wdown[i * width : (i + 1) * width, c : c + TILE])
-            r.t[:, c : c + TILE] = y
-        for start, half in chunks:
-            span = pl.ds(start, CHUNK)
-            y = r.t[span, :]
-            r.y[mb, span, :] = y.astype(low)
-            r.fout[job, span, :] = (r.m[span, :] + mod_row(mb, half, 5) * y).astype(low)
-
-        @pl.when(jnp.logical_or(jnp.logical_not(is_last), job < micro))
-        def _():
-            forward_copy(job, jnp.where(is_last, job + micro, job)).start()
 
         return carry
 
@@ -299,7 +341,7 @@
             shift_sum = jnp.zeros((8, width), wide)
             scale_sum = jnp.zeros((8, width), wide)
             gate_sum = jnp.zeros((8, width), wide)
-            for start in range(half * half_rows, (half + 1) * half_rows, CHUNK):
+            for start in half_chunks(half):
                 span = pl.ds(start, CHUNK)
                 da = r.t[span, :]
                 n = n_keep[mb_span(mb, start), :].astype(wide)
@@ -319,23 +361,31 @@
             r.dmod[mb, half, k_scale, :] = jnp.sum(scale_sum, axis=0)
             if k_scale == 4:
                 r.dmod[mb, half, 2, :] = jnp.sum(gate_sum, axis=0)
+            else:
+
+                @pl.when(jnp.logical_not(is_first))
+                def _():
+                    backward_copy(mb, half).start()
 
     def backward_job(mb, carry):
         g_s = r.h
         here = mb_rows(mb)
-
-        @pl.when(is_last)
-        def _():
-            g_s[...] = r.cot[mb].astype(wide)
-
-        @pl.when(jnp.logical_not(is_last))
-        def _():
-            backward_copy(mb).wait_recv()
-            g_s[...] = r.brecv[mb].astype(wide)
+        z_base = 0 if fused else micro * (ff // width)
 
         for half in range(halves):
+            rows_of = pl.ds(half * half_rows, half_rows)
+
+            @pl.when(is_last)
+            def _():
+                g_s[rows_of, :] = r.cot[mb, rows_of, :].astype(wide)
+
+            @pl.when(jnp.logical_not(is_last))
+            def _():
+                backward_copy(mb, half).wait_recv()
+                g_s[rows_of, :] = r.brecv[mb, rows_of, :].astype(wide)
+
             gate_sum = jnp.zeros((8, width), wide)
-            for start in range(half * half_rows, (half + 1) * half_rows, CHUNK):
+            for start in half_chunks(half):
                 span = pl.ds(start, CHUNK)
                 g = g_s[span, :]
                 gate_sum = gate_sum + fold(g * r.y[mb, span, :].astype(wide))
@@ -362,37 +412,52 @@
         dattn = r.dattn[mb]
         for c in range(0, width, TILE):
             r.do[:, c : c + TILE] = dot_nt(dattn, r.wa[c : c + TILE, qkv_width:]).astype(low)
-        bias = r.bias[mb]
-        for c in range(0, width, 128):
-            cols = [slice(i * width + c, i * width + c + 128) for i in range(3)]
-            q, k, v = [r.qkvo[here, cut] for cut in cols]
+        q_tag = r.tags[0, mb]
+        k_tag = r.tags[1, mb]
+
+        def pulls(c):
+            q, k, v = [r.qkvo[here, i * width + c : i * width + c + 128] for i in range(3)]
             do = r.do[:, c : c + 128]
+            k_wide = jnp.concatenate([k, k_tag], axis=1)
+            found = []
+            for mask in masks:
+                s = dot_nt(k_wide, jnp.concatenate([q * (mask * scale), q_tag], axis=1))
+                found.append((s, dot_nt(v * mask, do)))
+            return found, q, k, do
+
+        def push(c, found, q, k, do):
             parts = []
-            for mask in masks:
-                s = dot_nt(k, q * (mask * scale)) + bias
+            for s, dp in found:
                 e = jnp.exp(s - jnp.max(s, axis=0, keepdims=True))
                 p = e * (1.0 / jnp.sum(e, axis=0, keepdims=True))
-                dp = dot_nt(v * mask, do)
                 inner = jnp.sum(p * dp, axis=0, keepdims=True)
-                ds = (p * (dp - inner) * scale).astype(low)
+                ds = (p * (dp - inner)).astype(low)
                 parts.append((dot_tn(ds, k), dot_nn(ds, q), dot_nn(p.astype(low), do)))
-            for i in range(3):
-                r.qkvo[here, cols[i]] = jnp.where(first_lanes, parts[0][i], parts[1][i]).astype(
-                    low
+            for i, factor in enumerate((scale, scale, 1.0)):
+                both = jnp.where(first_lanes, parts[0][i], parts[1][i])
+                r.z[z_base + i, :, c : c + 128] = (both * factor).astype(low)
+
+        ahead = pulls(0)
+        for c in range(0, width, 128):
+            current = ahead
+            if c + 128 < width:
+                ahead = pulls(c + 128)
+            push(c, *current)
+        dqkv = [r.z[z_base + i] for i in range(3)]
+        for i in range(3):
+            r.qkvo[here, i * width : (i + 1) * width] = dqkv[i]
+        for c in range(0, width, TILE):
+            pulled = dot_nt(dqkv[0], r.wa[c : c + TILE, 0:width])
+            for i in range(1, 3):
+                pulled = pulled + dot_nt(
+                    dqkv[i], r.wa[c : c + TILE, i * width : (i + 1) * width]
                 )
-        dqkv = r.qkvo[here, 0:qkv_width]
-        for c in range(0, width, TILE):
-            r.t[:, c : c + TILE] = dot_nt(dqkv, r.wa[c : c + TILE, 0:qkv_width])
+            r.t[:, c : c + TILE] = pulled
 
         def after_attention(span, half, dh):
             r.gin[mb, span, :] = dh.astype(low)
 
         norm_backward(mb, 1, r.n1, r.r1, r.m, after_attention)
-
-        @pl.when(jnp.logical_not(is_first))
-        def _():
-            backward_copy(mb).start()
-
         return carry
 
     lax.fori_loop(0, micro, backward_job, 0)
@@ -400,17 +465,18 @@
     if fused:
         gradient_tail(r, section, z_at, core, member, remote, spread, relay, await_block)
 
-    for job in range(2 * micro):
-
-        @pl.when(jnp.logical_or(jnp.logical_not(is_last), job < micro))
-        def _():
-            forward_copy(job, job).wait_send()
-
-    for job in range(micro):
-
-        @pl.when(jnp.logical_not(is_first))
-        def _():
-            backward_copy(job).wait_send()
+    for half in range(halves):
+        for job in range(2 * micro):
+
+            @pl.when(jnp.logical_or(jnp.logical_not(is_last), job < micro))
+            def _():
+                forward_copy(job, job, half).wait_send()
+
+        for job in range(micro):
+
+            @pl.when(jnp.logical_not(is_first))
+            def _():
+                backward_copy(job, half).wait_send()
 
 
 def gradient_tail(r, section, z_at, core, member, remote, spread, relay, await_block):
@@ -474,12 +540,13 @@
             r.wa.at[share_rows(z, other), :], r.pa.at[z], r.pss.at[z], r.prs.at[z], partner
         )
 
-    for z in range(DEEP):
+    for z in (0, DEEP - 1, 1, DEEP - 2):
         pair_copy(z).start()
 
+    r.pdown[...] = jnp.zeros_like(r.pdown)
+    r.pin[...] = jnp.zeros_like(r.pin)
     for mb in range(micro):
         relay(r.a2, r.a2ss, r.a2rs, mb, False)
-    relay(r.dy, r.dyss, r.dyrs, 0, False)
 
     group = 2
 
@@ -507,12 +574,11 @@
     def sums(z):
         return r.qkvo.at[z * share : (z + 1) * share, :]
 
-    def sum_pair():
-        for z in range(DEEP):
-            pair_copy(z).wait_recv()
-            sums(z)[...] = (
-                r.wa[share_rows(z, core), :].astype(wide) + r.pa[z].astype(wide)
-            ).astype(low)
+    def sum_pair(z):
+        pair_copy(z).wait_recv()
+        sums(z)[...] = (r.wa[share_rows(z, core), :].astype(wide) + r.pa[z].astype(wide)).astype(
+            low
+        )
 
     def slot_of(z, direction):
         if direction > 0:
@@ -555,38 +621,38 @@
             add_slot(z, direction)
             line_copy(z, direction).start()
 
+    for at in range(DEEP):
+
+        @pl.when(z_at == at)
+        def _():
+            pl.semaphore_wait(r.free, (at > 0) + (at < DEEP - 1))
+
+    for z in (0, DEEP - 1, 1, DEEP - 2):
+        sum_pair(z)
+        if z > 0:
+            line_start(z, 1)
+        if z < DEEP - 1:
+            line_start(z, -1)
+
     def group_step(g, carry):
         @pl.when(g == 0)
         def _():
-            r.pdown[...] = jnp.zeros_like(r.pdown)
-            r.pin[...] = jnp.zeros_like(r.pin)
-
-        @pl.when(g == 2)
-        def _():
-            sum_pair()
-            for at in range(DEEP):
-
-                @pl.when(z_at == at)
-                def _():
-                    pl.semaphore_wait(r.free, (at > 0) + (at < DEEP - 1))
-
-            for z in (3, 2, 1):
-                line_start(z, 1)
-                line_start(DEEP - 1 - z, -1)
-            relay(r.dy, r.dyss, r.dyrs, 1, False)
-
-        mlp_group(lax.div(g, 2), lax.rem(g, 2) * group)
+            relay(r.dy, r.dyss, r.dyrs, 0, False)
 
         @pl.when(g == 2)
         def _():
             line_pass(3, 1, 1)
             line_pass(0, -1, 2)
+            relay(r.dy, r.dyss, r.dyrs, 1, False)
 
         @pl.when(g == 3)
         def _():
             line_pass(2, 1, 1)
             line_pass(1, -1, 2)
-
+            line_pass(3, 1, 2)
+            line_pass(0, -1, 1)
+
+        mlp_group(lax.div(g, 2), lax.rem(g, 2) * group)
         return carry
 
     lax.fori_loop(0, micro * DEEP // group, group_step, 0)
@@ -638,9 +704,6 @@
         def _():
             r.cols2[z] = total.astype(low)
             column_copy(z).start()
-
-    line_pass(3, 1, 2)
-    line_pass(0, -1, 1)
 
     def ada_pair():
         return remote(
@@ -732,7 +795,7 @@
     down_copy().wait_send()
 
 
-def run_chain(x, cot, mod, bias, feat, w_qkv, w_out, w_in, w_down, members):
+def run_chain(x, cot, mod, tags, feat, w_qkv, w_out, w_in, w_down, members):
     micro, rows, width = x.shape
     ff = w_in.shape[1]
     sections = lax.axis_size("section")
@@ -747,7 +810,7 @@
     def result(*shape):
         return jax.ShapeDtypeStruct(shape, wide)
 
-    names = ["x", "cot", "mod", "bias", "feat", "wqkv_h", "wout_h", "win_h", "wdown_h"]
+    names = ["x", "cot", "mod", "tags", "feat", "wqkv_h", "wout_h", "win_h", "wdown_h"]
     in_specs = [vmem] * 5 + [hbm] * 4
     stored = {
         "dmod": result(*mod.shape),
@@ -756,7 +819,7 @@
         "dattn": kept(micro, rows, width),
         "a2": kept(micro, DEEP if fused else 1, rows, width),
         "du": kept(micro * rows, ff),
-        "z": kept((1 if fused else micro) * (ff // width), rows, width),
+        "z": kept((1 if fused else micro + 1) * (ff // width), rows, width),
         "dy": kept(micro, DEEP if fused else 1, rows, width),
     }
     outs = {"fout": kept(2 * micro, rows, width), "gin": kept(micro, rows, width)}
@@ -785,10 +848,10 @@
         "frecv": pltpu.VMEM((2 * micro * rows, width), low),
         "brecv": pltpu.VMEM((micro, rows, width), low),
         "wsem": dma((4,)),
-        "fss": dma((2 * micro,)),
-        "frs": dma((2 * micro,)),
-        "bss": dma((micro,)),
-        "brs": dma((micro,)),
+        "fss": dma((2 * micro, rows // SHORT)),
+        "frs": dma((2 * micro, rows // SHORT)),
+        "bss": dma((micro, rows // SHORT)),
+        "brs": dma((micro, rows // SHORT)),
     }
     if fused:
         part = ff // DEEP
@@ -831,7 +894,7 @@
         compiler_params=pltpu.CompilerParams(
             collective_id=0, has_side_effects=True, vmem_limit_bytes=60 * 1024 * 1024
         ),
-    )(x, cot, mod, bias, feat, w_qkv, w_out, w_in, w_down)
+    )(x, cot, mod, tags, feat, w_qkv, w_out, w_in, w_down)
     return SimpleNamespace(**dict(zip(outs, values)))
 
 
@@ -861,7 +924,7 @@
         product(kept.a1, kept.qkvo[:, : 3 * width]),
         product(kept.qkvo[:, 3 * width :], kept.dattn),
         product(kept.a2, kept.du),
-        product(jnp.swapaxes(kept.z.reshape(micro, -1, rows, width), 1, 2), kept.dy),
+        product(jnp.swapaxes(kept.z.reshape(micro + 1, -1, rows, width)[:micro], 1, 2), kept.dy),
         grad_ada,
     )
 
@@ -881,13 +944,15 @@
     mod = jnp.pad(mod, ((0, 0), (0, 0), (0, 2), (0, 0)))
     feat = jnp.repeat(features.reshape(micro, halves, TEMB), 8, axis=1)
     slot_ids = jnp.where(is_long, 0, jnp.repeat(half_index, SHORT, axis=1))
-    same = slot_ids[:, :, None] == slot_ids[:, None, :]
-    bias = jnp.where(same, 0.0, -1e30).astype(wide)
+    spots = jnp.arange(128, dtype=jnp.int32)[None, None, :]
+    in_slot = slot_ids[:, :, None] == spots
+    barred = jnp.where(jnp.logical_or(in_slot, spots >= halves), 0.0, -1e30)
+    tags = jnp.stack([in_slot.astype(wide), barred]).astype(low)
     kept = run_chain(
         inputs.reshape(micro, rows, width),
         cotangent.reshape(micro, rows, width),
         mod,
-        bias,
+        tags,
         feat,
         w_qkv[0],
         w_out[0],

time: 339 us -> 281 us (0.83)
  Pallas kernels: 321 us -> 264 us
    pallas_call x1, Pallas kernels: 321 us -> 264 us  [run_chain(): pl.pallas_call(functools.partial(chain_kernel, names, sections, fused), o...]
where the time goes in v3:
time: 281 us; the launch traced here: 280 us
  Pallas kernels  264 us (94%)
  local copies, waits for them, and re-layouts  12.7 us (5%)
    pallas_call x1, Pallas kernels, run_chain(): pl.pallas_call(functools.partial(chain_kernel, names, sections, fused), o...  264 us
    unnamed x19, local copies, waits for them, and re-layouts  8.52 us

profile of v3, /device:TPU:0, one launch (start us, length us, event | category | flops | bytes accessed | tf_op | source)
XLA Modules:
  0.0 280.1 jit_solution(9103137722027694280)
XLA Ops:
  0.6 0.7 compare_bitcast_fusion
  1.3 0.8 slice_reduce_fusion
  2.1 0.8 convert_multiply_fusion
  2.9 0.1 fusion.1
  3.0 0.1 pad_maximum_fusion.1
  3.1 0.6 broadcast_bitcast_fusion.refs_4_
  3.7 0.1 select_convert_fusion
  3.9 0.1 convert_convert_fusion
  4.0 0.7 pad_maximum_fusion.refs_3_
  4.8 1.7 copy.18
  6.4 0.4 fusion.3
  6.9 0.7 pad.4.refs_2_
  7.5 263.6 %shard_map.144 = (bf16[4,256,768]{2,1,0:T(8,128)(2,1)}, bf16[2,256,768]{2,1,0:T(8,128)(2,1)}, f32[96,2304]{1,0:T(8,128)}, f32[96,768]{1,0:T(8,128)}, f32[96,3072...) custom-call(bf16[2,256,768]{2,1,0:T(8,128)(2,1)} %bitcast.42, bf16[2,256,768]{2,1,0:T(8,128)(2,1)} %bitcast.43, ...), custom_call_target="tpu_custom_call" | custom-call | tf_op jit(solution)/shard_map/pallas_call | solution.py:888
  271.1 2.1 slice.7
  273.3 0.9 copy.27
  274.1 0.6 copy-done.2
  274.7 0.9 copy.28
  275.6 0.2 copy-done.5
  275.8 0.7 copy.29
  276.6 1.0 copy.30
  277.6 0.7 copy-done
  278.3 1.0 copy.31
  279.3 0.1 copy-done.4
  279.4 0.7 copy.32
  (13 shorter events, 0.1 us)
Async XLA Ops:
  271.1 2.2 copy-start.3
  273.3 1.5 copy-start.2
  274.7 1.1 copy-start.5
  274.7 1.8 copy-start.1
  276.6 1.7 copy-start
  278.3 1.1 copy-start.4

commit v4 on v3

--- a/solution.py
+++ b/solution.py
@@ -16,6 +16,7 @@
 CHUNK = 32
 CORES = 2
 DEEP = 4
+INNER = (1, 2)
 norm_eps = 1e-06
 MESH = pl.DeviceIdType.MESH
 low = jnp.bfloat16
@@ -78,6 +79,15 @@
     is_first = section == 0
     is_last = section == sections - 1
 
+    maps = []
+    for k in range(6):
+        spot = pl.ds(k % 2 * TEMB, TEMB)
+        copy = pltpu.make_async_copy(
+            r.ada_h.at[:, pl.ds(k * width, width)], r.z.at[k // 2, spot, :], r.msem.at[k]
+        )
+        copy.start()
+        maps.append(copy)
+
     loads = []
     for index, (hbm, vmem) in enumerate(
         (
@@ -88,7 +98,8 @@
         )
     ):
         loads.append(pltpu.make_async_copy(hbm, vmem, r.wsem.at[index]))
-        loads[index].start()
+        if index == 0:
+            loads[index].start()
 
     barrier = pltpu.get_barrier_semaphore()
     greeted = [(left, member), (right, member)]
@@ -148,50 +159,22 @@
     scale = (width // HEADS) ** (-0.5)
     ones = jnp.ones((rows, 128), low)
 
-    near = (1, 2, -1, -2)
-
-    def spread_copy(buffer, send_sems, recv_sems, mb, k):
-        target = jnp.clip(z_at + near[k], 0, DEEP - 1)
-        return remote(
-            buffer.at[mb, z_at],
-            buffer.at[mb, z_at],
-            send_sems.at[mb, k],
-            recv_sems.at[mb, z_at],
-            (section, target * CORES + core),
-        )
-
     def spread(buffer, send_sems, recv_sems, mb, wait):
-        for k in range(len(near)):
-
-            @pl.when(jnp.logical_and(z_at + near[k] >= 0, z_at + near[k] < DEEP))
-            def _():
-                copy = spread_copy(buffer, send_sems, recv_sems, mb, k)
-                copy.wait_send() if wait else copy.start()
-
-    def relay(buffer, send_sems, recv_sems, mb, wait):
-        for at, source, target in ((2, 0, 3), (1, 3, 0)):
-
-            @pl.when(z_at == at)
+        for k, target in enumerate(INNER):
+
+            @pl.when(z_at != target)
             def _():
                 copy = remote(
-                    buffer.at[mb, source],
-                    buffer.at[mb, source],
-                    send_sems.at[mb, len(near)],
-                    recv_sems.at[mb, source],
+                    buffer.at[mb, z_at],
+                    buffer.at[mb, z_at],
+                    send_sems.at[mb, k],
+                    recv_sems.at[mb, z_at],
                     (section, target * CORES + core),
                 )
-                if wait:
-                    copy.wait_send()
-                else:
-                    copy.wait_recv()
-                    copy.start()
+                copy.wait_send() if wait else copy.start()
 
     def await_block(buffer, send_sems, recv_sems, mb, source):
-        relayed = jnp.logical_or(
-            jnp.logical_and(z_at == 2, source == 0), jnp.logical_and(z_at == 1, source == 3)
-        )
-
-        @pl.when(jnp.logical_and(z_at != source, jnp.logical_not(relayed)))
+        @pl.when(z_at != source)
         def _():
             remote(
                 buffer.at[mb, source],
@@ -215,6 +198,40 @@
             ).astype(low)
 
     r.dmod[...] = jnp.zeros_like(r.dmod)
+
+    for mb in range(micro):
+        long_row = (lane * 0 + r.long[0, mb]).astype(wide)
+        for half in range(halves):
+            here = (lane == 0).astype(wide)
+            there = (lane == half).astype(wide)
+            in_slot = long_row * here + (1.0 - long_row) * there
+            barred = (lane < halves).astype(wide) * (1.0 - in_slot) * -1e30
+            span = pl.ds(half * half_rows, half_rows)
+            r.tags[0, mb, span, :] = jnp.broadcast_to(in_slot, (half_rows, 128)).astype(low)
+            r.tags[1, mb, span, :] = jnp.broadcast_to(barred, (half_rows, 128)).astype(low)
+
+    pairs = [(mb, half) for mb in range(micro) for half in range(halves)]
+    row = lax.broadcasted_iota(jnp.int32, (8 * len(pairs), TEMB), 0)
+    steps = jnp.zeros((8 * len(pairs), TEMB), jnp.int32)
+    for i, (mb, half) in enumerate(pairs):
+        flag = r.long[0, mb]
+        chosen = flag * r.steps[0, mb, 0] + (1 - flag) * r.steps[0, mb, half]
+        steps = jnp.where(row // 8 == i, chosen, steps)
+    feature = lax.broadcasted_iota(jnp.int32, (8 * len(pairs), TEMB), 1)
+    half_width = TEMB // 2
+    position = lax.rem(feature, half_width).astype(wide)
+    angles = steps.astype(wide) * 0.1 * jnp.exp(position * (-math.log(10000.0) / half_width))
+    features = jnp.where(feature < half_width, jnp.sin(angles), jnp.cos(angles)).astype(low)
+    r.feat[...] = features.reshape(micro, 8 * halves, TEMB)
+    for copy in maps:
+        copy.wait()
+    for copy in loads[1:]:
+        copy.start()
+    for k in range(6):
+        spot = pl.ds(k % 2 * TEMB, TEMB)
+        found = dot_nn(features, r.z[k // 2, spot, :])
+        for i, (mb, half) in enumerate(pairs):
+            r.mod[mb, half, k : k + 1, :] = found[8 * i : 8 * i + 1, :]
 
     def forward_job(job, carry):
         mb = lax.rem(job, micro)
@@ -463,7 +480,7 @@
     lax.fori_loop(0, micro, backward_job, 0)
 
     if fused:
-        gradient_tail(r, section, z_at, core, member, remote, spread, relay, await_block)
+        gradient_tail(r, section, z_at, core, member, remote, spread, await_block)
 
     for half in range(halves):
         for job in range(2 * micro):
@@ -479,7 +496,7 @@
                 backward_copy(job, half).wait_send()
 
 
-def gradient_tail(r, section, z_at, core, member, remote, spread, relay, await_block):
+def gradient_tail(r, section, z_at, core, member, remote, spread, await_block):
     micro, rows, width = r.x.shape
     ff = r.win.shape[1]
     share = width // (DEEP * CORES)
@@ -522,16 +539,6 @@
         block = ref[...]
         return block.reshape(micro * rows, block.shape[-1])
 
-    a1_t = flat(r.a1).T
-    for c in range(0, qkv_width, TILE):
-        r.wa[:, c : c + TILE] = dot_nn(a1_t, r.qkvo[:, c : c + TILE]).astype(low)
-    o_t = r.qkvo[:, qkv_width:].T
-    dattn = flat(r.dattn)
-    for c in range(0, width, TILE):
-        r.wa[:, qkv_width + c : qkv_width + c + TILE] = dot_nn(
-            o_t, dattn[:, c : c + TILE]
-        ).astype(low)
-
     def share_rows(z, of_core):
         return pl.ds(pl.multiple_of((z * CORES + of_core) * share, share), share)
 
@@ -540,25 +547,47 @@
             r.wa.at[share_rows(z, other), :], r.pa.at[z], r.pss.at[z], r.prs.at[z], partner
         )
 
-    for z in (0, DEEP - 1, 1, DEEP - 2):
-        pair_copy(z).start()
-
-    r.pdown[...] = jnp.zeros_like(r.pdown)
-    r.pin[...] = jnp.zeros_like(r.pin)
-    for mb in range(micro):
-        relay(r.a2, r.a2ss, r.a2rs, mb, False)
-
+    a1_t = flat(r.a1).T
+    o_t = r.qkvo[:, qkv_width:].T
+    dattn = flat(r.dattn)
+    both = CORES * share
+    for pair in ((0, DEEP - 1), (1, DEEP - 2)):
+        a1_rows, o_rows = [
+            jnp.concatenate([side[z * both : (z + 1) * both] for z in pair], axis=0)
+            for side in (a1_t, o_t)
+        ]
+        for c in range(0, 4 * width, TILE):
+            if c < qkv_width:
+                found = dot_nn(a1_rows, r.qkvo[:, c : c + TILE])
+            else:
+                found = dot_nn(o_rows, dattn[:, c - qkv_width : c - qkv_width + TILE])
+            for i, z in enumerate(pair):
+                r.wa[z * both : (z + 1) * both, c : c + TILE] = found[
+                    i * both : (i + 1) * both
+                ].astype(low)
+        for z in pair:
+            pair_copy(z).start()
+
+    inner = jnp.logical_or(z_at == INNER[0], z_at == INNER[1])
+    edge = jnp.where(z_at == INNER[0], 0, DEEP - 1)
     group = 2
 
-    def mlp_group(mb, first):
+    def quarter(turn):
+        return jnp.where(turn == 0, edge, z_at)
+
+    def mlp_group(turn, mb, first):
         for step in range(group):
-            await_block(r.a2, r.a2ss, r.a2rs, mb, first + step)
-            await_block(r.dy, r.dyss, r.dyrs, mb, first + step)
+
+            @pl.when(turn == 0)
+            def _():
+                await_block(r.a2, r.a2ss, r.a2rs, mb, first + step)
+                await_block(r.dy, r.dyss, r.dyrs, mb, first + step)
+
         tokens = group * rows
         a2 = r.a2[mb, pl.ds(first, group)].reshape(tokens, width)
         dy = r.dy[mb, pl.ds(first, group)].reshape(tokens, width)
         for c in range(0, part, TILE):
-            at = pl.ds(pl.multiple_of(z_at * part + c, TILE), TILE)
+            at = pl.ds(pl.multiple_of(quarter(turn) * part + c, TILE), TILE)
             u = dot_nn(a2, r.win[:, at])
             dz = dot_nt(dy, r.wdown[at, :])
             active, slope = gelu_both(u)
@@ -569,7 +598,8 @@
         for c in range(0, width, TILE):
             r.pdown[:, c : c + TILE] += dot_nn(z_t, dy[:, c : c + TILE])
         for c in range(0, part, TILE):
-            r.pin[:, c : c + TILE] += dot_nn(a2_t, r.z[group:, :, c : c + TILE].reshape(tokens, TILE))
+            up = dot_nn(a2_t, r.z[group:, :, c : c + TILE].reshape(tokens, TILE))
+            r.pin[:, c : c + TILE] += up
 
     def sums(z):
         return r.qkvo.at[z * share : (z + 1) * share, :]
@@ -588,38 +618,27 @@
     def slot_ref(z, direction):
         return r.du.at[pl.ds(slot_of(z, direction) * share, share), :]
 
-    def line_copy(z, direction):
+    def line_copy(z, direction, piece):
         slot = slot_of(z, direction)
+        columns = pl.ds(piece * 2 * width, 2 * width)
         return remote(
-            sums(z),
-            slot_ref(z, direction),
-            r.lss.at[z],
-            r.lrs.at[slot],
+            sums(z).at[:, columns],
+            slot_ref(z, direction).at[:, columns],
+            r.lss.at[z, piece],
+            r.lrs.at[slot, piece],
             on_z(jnp.clip(z_at + direction, 0, DEEP - 1)),
         )
 
-    def passes(z, direction):
-        return z_at < z if direction > 0 else z_at > z
-
-    def takes(direction):
-        return z_at > 0 if direction > 0 else z_at < DEEP - 1
-
-    def add_slot(z, direction):
-        line_copy(z, direction).wait_recv()
-        sums(z)[...] = (
-            sums(z)[...].astype(wide) + slot_ref(z, direction)[...].astype(wide)
-        ).astype(low)
-
-    def line_start(z, direction):
-        @pl.when(jnp.logical_and(passes(z, direction), jnp.logical_not(takes(direction))))
-        def _():
-            line_copy(z, direction).start()
-
-    def line_pass(z, direction, at):
+    def line_pass(z, direction, at, piece):
         @pl.when(z_at == at)
         def _():
-            add_slot(z, direction)
-            line_copy(z, direction).start()
+            line_copy(z, direction, piece).wait_recv()
+            columns = slice(piece * 2 * width, (piece + 1) * 2 * width)
+            sums(z)[:, columns] = (
+                sums(z)[:, columns].astype(wide)
+                + slot_ref(z, direction)[:, columns].astype(wide)
+            ).astype(low)
+            line_copy(z, direction, piece).start()
 
     for at in range(DEEP):
 
@@ -627,83 +646,165 @@
         def _():
             pl.semaphore_wait(r.free, (at > 0) + (at < DEEP - 1))
 
-    for z in (0, DEEP - 1, 1, DEEP - 2):
-        sum_pair(z)
-        if z > 0:
-            line_start(z, 1)
-        if z < DEEP - 1:
-            line_start(z, -1)
-
-    def group_step(g, carry):
-        @pl.when(g == 0)
-        def _():
-            relay(r.dy, r.dyss, r.dyrs, 0, False)
-
-        @pl.when(g == 2)
-        def _():
-            line_pass(3, 1, 1)
-            line_pass(0, -1, 2)
-            relay(r.dy, r.dyss, r.dyrs, 1, False)
-
-        @pl.when(g == 3)
-        def _():
-            line_pass(2, 1, 1)
-            line_pass(1, -1, 2)
-            line_pass(3, 1, 2)
-            line_pass(0, -1, 1)
-
-        mlp_group(lax.div(g, 2), lax.rem(g, 2) * group)
+    far_first = (0, DEEP - 1, 1, DEEP - 2)
+
+    @pl.when(jnp.logical_not(inner))
+    def _():
+        for z in far_first:
+            sum_pair(z)
+
+        def queue(direction):
+            order = [(z, piece) for z in (3, 2, 1) for piece in range(2)]
+            if direction < 0:
+                order = [(DEEP - 1 - z, piece) for z, piece in order]
+            for i, (z, piece) in enumerate(order):
+                if i >= 2:
+                    before, half = order[i - 2]
+                    line_copy(before, direction, half).wait_send()
+                line_copy(z, direction, piece).start()
+
+        @pl.when(z_at == 0)
+        def _():
+            queue(1)
+
+        @pl.when(z_at == DEEP - 1)
+        def _():
+            queue(-1)
+
+    pl.semaphore_wait(r.done, 1)
+
+    def staged(kind, turn):
+        return pl.ds((kind * 2 + turn) * part, part)
+
+    def landing(turn):
+        return r.frecv if turn == 0 else r.land2
+
+    def down_copy(turn):
+        return remote(
+            (r.n1, r.n2)[turn].at[pl.ds(0, half_part), :],
+            landing(turn).at[pl.ds(DEEP * share, half_part), :],
+            r.mss.at[turn, DEEP],
+            r.mrs.at[turn, DEEP],
+            partner,
+        )
+
+    def up_copy(turn, z):
+        return remote(
+            r.pa.at[z, :, staged(0, turn)],
+            landing(turn).at[pl.ds(z * share, share), :],
+            r.mss.at[turn, z],
+            r.mrs.at[turn, z],
+            partner,
+        )
+
+    def column_copy(turn, z):
+        return remote(
+            r.pa.at[z, :, staged(1, turn)],
+            r.land.at[quarter(turn)],
+            r.css.at[turn, z],
+            r.crs.at[quarter(turn)],
+            on_z(z),
+        )
+
+    def edge_copy():
+        return remote(
+            r.slice, r.frecv.at[pl.ds(0, half_part), :], r.ess.at[0], r.ers.at[0], on_z(edge)
+        )
+
+    def half_rows_of(which):
+        return pl.ds(pl.multiple_of(which * half_part, half_part), half_part)
+
+    def down_rows(z):
+        return pl.ds(pl.multiple_of(core * half_part + z * share, share), share)
+
+    def exchange(turn):
+        for z in range(DEEP):
+            r.pa[z, :, staged(0, turn)] = r.pin[share_rows(z, other), :].astype(low)
+            up_copy(turn, z).start()
+        (r.n1, r.n2)[turn][0:half_part, :] = r.pdown[half_rows_of(other), :].astype(low)
+        down_copy(turn).start()
+        for z in range(DEEP):
+            r.wa[share_rows(z, core), 0:part] = r.pin[share_rows(z, core), :].astype(low)
+            r.wa[share_rows(z, core), part : 2 * part] = r.pdown[down_rows(z), :].astype(low)
+
+    def finish_quarter(turn):
+        for z in range(DEEP):
+            up_copy(turn, z).wait_recv()
+            arrived = landing(turn)[z * share : (z + 1) * share, :].astype(wide)
+            total = r.wa[share_rows(z, core), 0:part].astype(wide) + arrived
+
+            @pl.when(z_at == z)
+            def _():
+                to = pl.ds(pl.multiple_of(quarter(turn) * part, part), part)
+                r.g_up[:, to] = total
+
+            @pl.when(z_at != z)
+            def _():
+                r.pa[z, :, staged(1, turn)] = total.astype(low)
+                column_copy(turn, z).start()
+
+        down_copy(turn).wait_recv()
+        for z in range(DEEP):
+            arrived = landing(turn)[(DEEP + z) * share : (DEEP + z + 1) * share, :].astype(wide)
+            total = r.wa[share_rows(z, core), part : 2 * part].astype(wide) + arrived
+            if turn == 0:
+                r.slice[z * share : (z + 1) * share, :] = total.astype(low)
+            else:
+                r.g_down[z * share : (z + 1) * share, :] = total
+        if turn == 0:
+            edge_copy().start()
+
+    def clear():
+        r.pdown[...] = jnp.zeros_like(r.pdown)
+        r.pin[...] = jnp.zeros_like(r.pin)
+
+    groups = micro * DEEP // group
+
+    def group_step(step, carry):
+        turn = lax.div(step, groups)
+        at = lax.rem(step, groups)
+
+        @pl.when(step == DEEP // group)
+        def _():
+            for z in far_first:
+                sum_pair(z)
+
+        @pl.when(step == groups)
+        def _():
+            exchange(0)
+            clear()
+            line_pass(3, 1, 1, 0)
+            line_pass(0, -1, 2, 0)
+
+        @pl.when(step == groups + 1)
+        def _():
+            finish_quarter(0)
+            line_pass(3, 1, 1, 1)
+            line_pass(0, -1, 2, 1)
+
+        @pl.when(step == groups + 2)
+        def _():
+            line_pass(3, 1, 2, 0)
+            line_pass(0, -1, 1, 0)
+            line_pass(2, 1, 1, 0)
+            line_pass(1, -1, 2, 0)
+
+        @pl.when(step == groups + 3)
+        def _():
+            line_pass(3, 1, 2, 1)
+            line_pass(0, -1, 1, 1)
+            line_pass(2, 1, 1, 1)
+            line_pass(1, -1, 2, 1)
+
+        place = lax.rem(at, DEEP // group) * group
+        mlp_group(turn, lax.div(at, DEEP // group), jnp.where(z_at == INNER[0], place, group - place))
         return carry
 
-    lax.fori_loop(0, micro * DEEP // group, group_step, 0)
-
-    def down_copy():
-        return remote(
-            r.n1.at[pl.ds(0, half_part), :],
-            r.frecv.at[pl.ds(width // CORES, half_part), :],
-            r.mss.at[DEEP],
-            r.mrs.at[DEEP],
-            partner,
-        )
-
-    def up_copy(z):
-        return remote(
-            r.cols.at[z],
-            r.frecv.at[pl.ds(z * share, share), :],
-            r.mss.at[z],
-            r.mrs.at[z],
-            partner,
-        )
-
-    pl.semaphore_wait(r.done, 1)
-    for z in range(DEEP):
-        r.cols[z] = r.pin[share_rows(z, other), :].astype(low)
-        up_copy(z).start()
-    r.n1[0:half_part, :] = r.pdown[
-        pl.ds(pl.multiple_of(other * half_part, half_part), half_part), :
-    ].astype(low)
-    down_copy().start()
-
-    def column_copy(z):
-        return remote(
-            r.cols2.at[z], r.land.at[z_at], r.css.at[z], r.crs.at[z_at], on_z(z)
-        )
-
-    def part_columns(z):
-        return pl.ds(pl.multiple_of(z * part, part), part)
-
-    for z in range(DEEP):
-        up_copy(z).wait_recv()
-        total = r.pin[share_rows(z, core), :] + r.frecv[z * share : (z + 1) * share, :].astype(wide)
-
-        @pl.when(z_at == z)
-        def _():
-            r.g_up[:, part_columns(z)] = total
-
-        @pl.when(z_at != z)
-        def _():
-            r.cols2[z] = total.astype(low)
-            column_copy(z).start()
+    @pl.when(inner)
+    def _():
+        clear()
+        lax.fori_loop(0, 2 * groups, group_step, 0)
+        exchange(1)
 
     def ada_pair():
         return remote(
@@ -724,12 +825,6 @@
             ).wait_recv()
 
     ada_pair().start()
-
-    down_copy().wait_recv()
-    own_half = pl.ds(pl.multiple_of(core * half_part, half_part), half_part)
-    r.g_down[...] = r.pdown[own_half, :] + r.frecv[
-        width // CORES : width // CORES + half_part, :
-    ].astype(wide)
 
     ada_other().wait_recv()
     entries = CORES * DEEP * micro * r.feat.shape[1]
@@ -745,13 +840,16 @@
         chosen = jnp.where(which == k, spreads, 0.0).astype(low)
         r.g_ada[:, k * width : (k + 1) * width] = dot_nn(chosen, gathered)
 
+    @pl.when(inner)
+    def _():
+        finish_quarter(1)
+
     def finish(z):
-        for direction in (1, -1):
-
-            @pl.when(takes(direction))
-            def _():
-                if (direction > 0 and z > 0) or (direction < 0 and z < DEEP - 1):
-                    line_copy(z, direction).wait_recv()
+        for piece in range(2):
+            if z > 0:
+                line_copy(z, 1, piece).wait_recv()
+            if z < DEEP - 1:
+                line_copy(z, -1, piece).wait_recv()
         total = sums(z)[...].astype(wide)
         if z > 0:
             total = total + slot_ref(z, 1)[...].astype(wide)
@@ -766,36 +864,52 @@
         def _():
             finish(z)
 
-    for z in range(DEEP):
-
-        @pl.when(z_at != z)
+    for q in range(DEEP):
+
+        @pl.when(z_at != INNER[q // 2])
         def _():
             remote(
-                r.cols2.at[z], r.land.at[z], r.css.at[z], r.crs.at[z], on_z(z)
+                r.pa.at[0, :, staged(1, 0)], r.land.at[q], r.css.at[0, 0], r.crs.at[q], partner
             ).wait_recv()
-            r.g_up[:, z * part : (z + 1) * part] = r.land[z].astype(wide)
+            r.g_up[:, q * part : (q + 1) * part] = r.land[q].astype(wide)
+
+    @pl.when(jnp.logical_not(inner))
+    def _():
+        edge_copy().wait_recv()
+        r.g_down[...] = r.frecv[0:half_part, :].astype(wide)
 
     for mb in range(micro):
         spread(r.a2, r.a2ss, r.a2rs, mb, True)
         spread(r.dy, r.dyss, r.dyrs, mb, True)
-        relay(r.a2, r.a2ss, r.a2rs, mb, True)
-        relay(r.dy, r.dyss, r.dyrs, mb, True)
     for away in range(1, DEEP):
         ada_copy(away).wait_send()
     ada_pair().wait_send()
     for z in range(DEEP):
         pair_copy(z).wait_send()
-        up_copy(z).wait_send()
-
-        @pl.when(z_at != z)
-        def _():
-            column_copy(z).wait_send()
-            line_copy(z, 1 if z > 0 else -1).wait_send()
-
-    down_copy().wait_send()
-
-
-def run_chain(x, cot, mod, tags, feat, w_qkv, w_out, w_in, w_down, members):
+
+        unsent = inner
+        if z in (1, 2):
+            unsent = jnp.logical_or(inner, z_at == (0 if z == 1 else DEEP - 1))
+
+        @pl.when(jnp.logical_and(unsent, z_at != z))
+        def _():
+            for piece in range(2):
+                line_copy(z, 1 if z > 0 else -1, piece).wait_send()
+
+    @pl.when(inner)
+    def _():
+        edge_copy().wait_send()
+        for turn in range(2):
+            down_copy(turn).wait_send()
+            for z in range(DEEP):
+                up_copy(turn, z).wait_send()
+
+                @pl.when(z_at != z)
+                def _():
+                    column_copy(turn, z).wait_send()
+
+
+def run_chain(x, cot, long_count, timesteps, ada_weight, w_qkv, w_out, w_in, w_down, members):
     micro, rows, width = x.shape
     ff = w_in.shape[1]
     sections = lax.axis_size("section")
@@ -810,10 +924,12 @@
     def result(*shape):
         return jax.ShapeDtypeStruct(shape, wide)
 
-    names = ["x", "cot", "mod", "tags", "feat", "wqkv_h", "wout_h", "win_h", "wdown_h"]
-    in_specs = [vmem] * 5 + [hbm] * 4
+    halves = rows // SHORT
+    smem = pl.BlockSpec(memory_space=pltpu.SMEM)
+    names = ["long", "steps", "x", "cot", "ada_h", "wqkv_h", "wout_h", "win_h", "wdown_h"]
+    in_specs = [smem] * 2 + [vmem] * 2 + [hbm] * 5
     stored = {
-        "dmod": result(*mod.shape),
+        "dmod": result(micro, halves, 8, width),
         "a1": kept(micro, rows, width),
         "qkvo": kept(micro * rows, 4 * width),
         "dattn": kept(micro, rows, width),
@@ -836,6 +952,10 @@
         "wa": pltpu.VMEM((width, 4 * width), low),
         "win": pltpu.VMEM((width, ff), low),
         "wdown": pltpu.VMEM((ff, width), low),
+        "mod": pltpu.VMEM((micro, halves, 8, width), wide),
+        "tags": pltpu.VMEM((2, micro, rows, 128), low),
+        "feat": pltpu.VMEM((micro, 8 * halves, TEMB), low),
+        "msem": dma((6,)),
         "h": pltpu.VMEM((rows, width), wide),
         "m": pltpu.VMEM((rows, width), wide),
         "t": pltpu.VMEM((rows, width), wide),
@@ -862,25 +982,27 @@
                 "pa": pltpu.VMEM((DEEP, share, 4 * width), low),
                 "pdown": pltpu.VMEM((part, width), wide),
                 "pin": pltpu.VMEM((width, part), wide),
-                "cols": pltpu.VMEM((DEEP, share, part), low),
-                "cols2": pltpu.VMEM((DEEP, share, part), low),
+                "land2": pltpu.VMEM((DEEP * share + part // CORES, part), low),
+                "slice": pltpu.VMEM((part // CORES, width), low),
                 "land": pltpu.VMEM((DEEP, share, part), low),
-                "ada": pltpu.VMEM((CORES, DEEP, micro, feat.shape[1], width + TEMB), low),
+                "ada": pltpu.VMEM((CORES, DEEP, micro, 8 * halves, width + TEMB), low),
                 "free": pltpu.SemaphoreType.REGULAR,
                 "done": pltpu.SemaphoreType.REGULAR,
-                "a2ss": dma((micro, 5)),
+                "a2ss": dma((micro, len(INNER))),
                 "a2rs": dma((micro, DEEP)),
-                "dyss": dma((micro, 5)),
+                "dyss": dma((micro, len(INNER))),
                 "dyrs": dma((micro, DEEP)),
                 "adass": dma((DEEP,)),
                 "adars": dma((DEEP + 1,)),
                 "pss": dma((DEEP,)),
                 "prs": dma((DEEP,)),
-                "lss": dma((DEEP,)),
-                "lrs": dma((5,)),
-                "mss": dma((DEEP + 1,)),
-                "mrs": dma((DEEP + 1,)),
-                "css": dma((DEEP,)),
+                "lss": dma((DEEP, 2)),
+                "lrs": dma((5, 2)),
+                "mss": dma((2, DEEP + 1)),
+                "mrs": dma((2, DEEP + 1)),
+                "ess": dma((1,)),
+                "ers": dma((1,)),
+                "css": dma((2, DEEP)),
                 "crs": dma((DEEP,)),
             }
         )
@@ -894,7 +1016,7 @@
         compiler_params=pltpu.CompilerParams(
             collective_id=0, has_side_effects=True, vmem_limit_bytes=60 * 1024 * 1024
         ),
-    )(x, cot, mod, tags, feat, w_qkv, w_out, w_in, w_down)
+    )(long_count, timesteps, x, cot, ada_weight, w_qkv, w_out, w_in, w_down)
     return SimpleNamespace(**dict(zip(outs, values)))
 
 
@@ -935,25 +1057,12 @@
     rows = inputs.shape[0] // micro
     halves = rows // SHORT
     members = lax.axis_size("dp")
-    is_long = (long_count[0] == 1)[:, None]
-    half_index = jnp.arange(halves, dtype=jnp.int32)[None, :]
-    half_steps = jnp.where(is_long, timesteps[0][:, :1], timesteps[0][:, :halves])
-    features = time_features(half_steps.reshape(-1)).astype(low)
-    mod = jnp.dot(features, ada_weight[0], preferred_element_type=wide)
-    mod = mod.reshape(micro, halves, 6, width)
-    mod = jnp.pad(mod, ((0, 0), (0, 0), (0, 2), (0, 0)))
-    feat = jnp.repeat(features.reshape(micro, halves, TEMB), 8, axis=1)
-    slot_ids = jnp.where(is_long, 0, jnp.repeat(half_index, SHORT, axis=1))
-    spots = jnp.arange(128, dtype=jnp.int32)[None, None, :]
-    in_slot = slot_ids[:, :, None] == spots
-    barred = jnp.where(jnp.logical_or(in_slot, spots >= halves), 0.0, -1e30)
-    tags = jnp.stack([in_slot.astype(wide), barred]).astype(low)
     kept = run_chain(
         inputs.reshape(micro, rows, width),
         cotangent.reshape(micro, rows, width),
-        mod,
-        tags,
-        feat,
+        long_count,
+        timesteps,
+        ada_weight[0],
         w_qkv[0],
         w_out[0],
         w_in[0],
@@ -961,12 +1070,51 @@
         members,
     )
     if members == DEEP * CORES:
-        grads = (kept.g_qkv, kept.g_out, kept.g_up, kept.g_down, kept.g_ada)
+        hidden, grad_in, *grads = handed_over(
+            (kept.fout, kept.gin, kept.g_qkv, kept.g_out, kept.g_up, kept.g_down, kept.g_ada)
+        )
     else:
+        is_long = (long_count[0] == 1)[:, None]
+        half_steps = jnp.where(is_long, timesteps[0][:, :1], timesteps[0][:, :halves])
+        features = time_features(half_steps.reshape(-1)).astype(low)
         grads = summed_apart(kept, features, micro, rows, width)
-    hidden_out = kept.fout[micro:].reshape(1, micro * rows, width)
-    grad_in = kept.gin.reshape(1, micro * rows, width)
+        hidden, grad_in = kept.fout[micro:], kept.gin
+    hidden_out = hidden.reshape(1, micro * rows, width)
+    grad_in = grad_in.reshape(1, micro * rows, width)
     return (hidden_out, grad_in) + tuple(grad[None] for grad in grads)
+
+
+def handed_over(results):
+    micro = results[1].shape[0]
+
+    def kernel(*refs):
+        count = len(results)
+        sources, targets, holds = [refs[i * count : (i + 1) * count] for i in range(3)]
+        sems = refs[-1]
+        arrivals, departures = [], []
+        for i in range(count):
+            source = sources[i].at[pl.ds(micro, micro)] if i == 0 else sources[i]
+            arrivals.append(pltpu.make_async_copy(source, holds[i], sems.at[0, i]))
+            departures.append(pltpu.make_async_copy(holds[i], targets[i], sems.at[1, i]))
+            arrivals[i].start()
+        for i in range(count):
+            arrivals[i].wait()
+            departures[i].start()
+        for copy in departures:
+            copy.wait()
+
+    shapes = [jax.ShapeDtypeStruct(value.shape, value.dtype) for value in results]
+    shapes[0] = jax.ShapeDtypeStruct((micro,) + results[0].shape[1:], results[0].dtype)
+    anywhere = pl.BlockSpec(memory_space=pl.ANY)
+    return pl.pallas_call(
+        kernel,
+        out_shape=tuple(shapes),
+        in_specs=[anywhere] * len(results),
+        out_specs=[anywhere] * len(results),
+        scratch_shapes=[pltpu.VMEM(shape.shape, shape.dtype) for shape in shapes]
+        + [pltpu.SemaphoreType.DMA((2, len(results)))],
+        compiler_params=pltpu.CompilerParams(vmem_limit_bytes=60 * 1024 * 1024),
+    )(*results)
 
 
 def solution(mesh):

time: 281 us -> 262 us (0.932)
  local copies, waits for them, and re-layouts: 12.7 us -> 0 us
  Pallas kernels: 264 us -> 261 us
    unnamed x19 -> x0, local copies, waits for them, and re-layouts: 8.52 us -> none
    pallas_call x1, Pallas kernels: 264 us -> 257 us  [run_chain(): pl.pallas_call(functools.partial(chain_kernel, names, sections, fused), o...]
    pallas_call x0 -> x1, Pallas kernels: none -> 4.66 us  [handed_over(): pl.pallas_call(kernel, out_shape=tuple(shapes), in_specs=[anywhere] * len...]
    slice x2 -> x0, local copies, waits for them, and re-layouts: 2.93 us -> none  [the longest x1 2.14 us: on_device(): hidden_out = kept.fout[micro:].reshape(1, micro * rows, width)]
where the time goes in v4:
time: 262 us
  Pallas kernels  261 us (100%)
    pallas_call x1, Pallas kernels, run_chain(): pl.pallas_call(functools.partial(chain_kernel, names, sections, fused), o...  257 us

profile of v4, /device:TPU:0, one launch (start us, length us, event | category | flops | bytes accessed | tf_op | source)
XLA Modules:
  0.0 262.0 jit_solution(13585925306287602086)
XLA Ops:
  0.6 256.5 %shard_map.144 = (bf16[4,256,768]{2,1,0:T(8,128)(2,1)}, bf16[2,256,768]{2,1,0:T(8,128)(2,1)}, f32[96,2304]{1,0:T(8,128)}, f32[96,768]{1,0:T(8,128)}, f32[96,3072...) custom-call(s32[1,2]{1,0:T(1,128)} %refs_0_.1, s32[1,2,2]{2,1,0:T(2,128)} %refs_1_.1, ...), custom_call_target="tpu_custom_call" | custom-call | tf_op jit(solution)/shard_map/pallas_call | solution.py:1010
  257.2 4.7 %shard_map.145 = (bf16[2,256,768]{2,1,0:T(8,128)(2,1)}, bf16[2,256,768]{2,1,0:T(8,128)(2,1)}, f32[96,2304]{1,0:T(8,128)}, f32[96,768]{1,0:T(8,128)}, f32[96,3072...) custom-call(bf16[4,256,768]{2,1,0:T(8,128)(2,1)} %get-tuple-element.21.refs_0_, ...), custom_call_target="tpu_custom_call" | custom-call | tf_op jit(solution)/shard_map/pallas_call | solution.py:1109

commit v5 on v4

--- a/solution.py
+++ b/solution.py
@@ -102,9 +102,9 @@
             loads[index].start()
 
     barrier = pltpu.get_barrier_semaphore()
-    greeted = [(left, member), (right, member)]
+    partner = (section, z_at * CORES + 1 - core)
+    greeted = [(left, member), (right, member), partner]
     if fused:
-        greeted.append((section, z_at * CORES + 1 - core))
         for away in range(1, DEEP):
             greeted.append((section, lax.rem(z_at + away, DEEP) * CORES + core))
     for target in greeted:
@@ -236,6 +236,12 @@
     def forward_job(job, carry):
         mb = lax.rem(job, micro)
         here = mb_rows(mb)
+        opening = jnp.logical_and(is_first, job == 0)
+
+        @pl.when(jnp.logical_and(opening, core == 0))
+        def _():
+            pl.semaphore_wait(r.turn, 1)
+
         z_base = 0 if fused else mb * (ff // width)
 
         def wait_load(index):
@@ -298,6 +304,10 @@
             if c + 128 < width:
                 ahead = scores(c + 128)
             mix(c, *current)
+        @pl.when(jnp.logical_and(opening, core == 1))
+        def _():
+            pl.semaphore_signal(r.turn, inc=1, device_id=partner, device_id_type=MESH)
+
         wait_load(1)
         wait_load(2)
         wait_load(3)
@@ -336,6 +346,7 @@
             def _():
                 forward_copy(job, jnp.where(is_last, job + micro, job), half).start()
 
+
         if fused:
 
             @pl.when(job >= micro)
@@ -349,7 +360,7 @@
         pl.semaphore_signal(
             r.done,
             inc=1,
-            device_id=(section, z_at * CORES + 1 - core),
+            device_id=partner,
             device_id_type=MESH,
         )
 
@@ -955,6 +966,7 @@
         "mod": pltpu.VMEM((micro, halves, 8, width), wide),
         "tags": pltpu.VMEM((2, micro, rows, 128), low),
         "feat": pltpu.VMEM((micro, 8 * halves, TEMB), low),
+        "turn": pltpu.SemaphoreType.REGULAR,
         "msem": dma((6,)),
         "h": pltpu.VMEM((rows, width), wide),
         "m": pltpu.VMEM((rows, width), wide),

time: 262 us -> 252 us (0.962)
  Pallas kernels: 261 us -> 251 us
    pallas_call x1, Pallas kernels: 257 us -> 246 us  [run_chain(): pl.pallas_call(functools.partial(chain_kernel, names, sections, fused), o...]
where the time goes in v5:
time: 252 us
  Pallas kernels  251 us (100%)
    pallas_call x1, Pallas kernels, run_chain(): pl.pallas_call(functools.partial(chain_kernel, names, sections, fused), o...  246 us

profile of v5, /device:TPU:0, one launch (start us, length us, event | category | flops | bytes accessed | tf_op | source)
XLA Modules:
  0.0 251.8 jit_solution(5960557929829552316)
XLA Ops:
  0.6 246.3 %shard_map.144 = (bf16[4,256,768]{2,1,0:T(8,128)(2,1)}, bf16[2,256,768]{2,1,0:T(8,128)(2,1)}, f32[96,2304]{1,0:T(8,128)}, f32[96,768]{1,0:T(8,128)}, f32[96,3072...) custom-call(s32[1,2]{1,0:T(1,128)} %refs_0_.1, s32[1,2,2]{2,1,0:T(2,128)} %refs_1_.1, ...), custom_call_target="tpu_custom_call" | custom-call | tf_op jit(solution)/shard_map/pallas_call | solution.py:1022
  247.0 4.7 %shard_map.145 = (bf16[2,256,768]{2,1,0:T(8,128)(2,1)}, bf16[2,256,768]{2,1,0:T(8,128)(2,1)}, f32[96,2304]{1,0:T(8,128)}, f32[96,768]{1,0:T(8,128)}, f32[96,3072...) custom-call(bf16[4,256,768]{2,1,0:T(8,128)(2,1)} %get-tuple-element.21.refs_0_, ...), custom_call_target="tpu_custom_call" | custom-call | tf_op jit(solution)/shard_map/pallas_call | solution.py:1121

commit v6 on v5

--- a/solution.py
+++ b/solution.py
@@ -13,7 +13,7 @@
 TEMB = 128
 SHORT = 128
 TILE = 256
-CHUNK = 32
+CHUNK = 64
 CORES = 2
 DEEP = 4
 INNER = (1, 2)
@@ -184,10 +184,10 @@
                 (section, member),
             ).wait_recv()
 
-    def norm_forward(src, mb, half, k_shift, k_scale, n_keep, r_keep, out):
+    def norm_forward(values, mb, half, k_shift, k_scale, n_keep, r_keep, out):
         for start in half_chunks(half):
             span = pl.ds(start, CHUNK)
-            v = src[span, :]
+            v = values(span)
             centered = v - jnp.mean(v, axis=-1, keepdims=True)
             inverse = lax.rsqrt(jnp.mean(centered * centered, axis=-1, keepdims=True) + norm_eps)
             n = centered * inverse
@@ -251,27 +251,43 @@
 
         for half in range(halves):
             span = pl.ds(half * half_rows, half_rows)
-            arrived = pl.ds(
-                pl.multiple_of(job * rows + half * half_rows, half_rows), half_rows
-            )
 
             @pl.when(jnp.logical_or(jnp.logical_not(is_first), job >= micro))
             def _():
                 forward_copy(job, job, half).wait_recv()
 
+            def entering(part_span):
+                begin = part_span.start
+                given = pl.ds(pl.multiple_of(job * rows + begin, CHUNK), CHUNK)
+                return given
+
             @pl.when(jnp.logical_and(is_first, job < micro))
             def _():
-                r.h[span, :] = r.x[mb, span, :].astype(wide)
+                def values(at):
+                    h = r.x[mb, at, :].astype(wide)
+                    r.h[at, :] = h
+                    return h
+
+                norm_forward(values, mb, half, 0, 1, r.n1, r.r1, r.a1.at[mb])
 
             @pl.when(jnp.logical_and(is_first, job >= micro))
             def _():
-                r.h[span, :] = r.x[mb, span, :].astype(wide) + r.frecv[arrived, :].astype(wide)
+                def values(at):
+                    h = r.x[mb, at, :].astype(wide) + r.frecv[entering(at), :].astype(wide)
+                    r.h[at, :] = h
+                    return h
+
+                norm_forward(values, mb, half, 0, 1, r.n1, r.r1, r.a1.at[mb])
 
             @pl.when(jnp.logical_not(is_first))
             def _():
-                r.h[span, :] = r.frecv[arrived, :].astype(wide)
-
-            norm_forward(r.h, mb, half, 0, 1, r.n1, r.r1, r.a1.at[mb])
+                def values(at):
+                    h = r.frecv[entering(at), :].astype(wide)
+                    r.h[at, :] = h
+                    return h
+
+                norm_forward(values, mb, half, 0, 1, r.n1, r.r1, r.a1.at[mb])
+
             if half == 0:
                 wait_load(0)
             a1 = r.a1[mb, span, :]
@@ -318,12 +334,14 @@
             o = r.do[span, :]
             for c in range(0, width, TILE):
                 r.t[span, c : c + TILE] = dot_nn(o, r.wa[:, qkv_width + c : qkv_width + c + TILE])
-            for start in half_chunks(half):
-                part = pl.ds(start, CHUNK)
-                attn = r.t[part, :]
-                r.dattn[mb, part, :] = attn.astype(low)
-                r.m[part, :] = r.h[part, :] + mod_row(mb, half, 2) * attn
-            norm_forward(r.m, mb, half, 3, 4, r.n2, r.r2, r.a2.at[mb, own])
+            def residual(at):
+                attn = r.t[at, :]
+                r.dattn[mb, at, :] = attn.astype(low)
+                m = r.h[at, :] + mod_row(mb, half, 2) * attn
+                r.m[at, :] = m
+                return m
+
+            norm_forward(residual, mb, half, 3, 4, r.n2, r.r2, r.a2.at[mb, own])
             a2 = r.a2[mb, own, span, :]
             for c in range(0, ff, TILE):
                 u = dot_nn(a2, r.win[:, c : c + TILE])

time: 252 us -> 252 us (level)
  no operation moved by 1% of the time
where the time goes in v6:
time: 252 us
  Pallas kernels  251 us (100%)
    pallas_call x1, Pallas kernels, run_chain(): pl.pallas_call(functools.partial(chain_kernel, names, sections, fused), o...  247 us

profile of v6, /device:TPU:0, one launch (start us, length us, event | category | flops | bytes accessed | tf_op | source)
XLA Modules:
  0.0 252.3 jit_solution(16077477902588933690)
XLA Ops:
  0.6 246.8 %shard_map.144 = (bf16[4,256,768]{2,1,0:T(8,128)(2,1)}, bf16[2,256,768]{2,1,0:T(8,128)(2,1)}, f32[96,2304]{1,0:T(8,128)}, f32[96,768]{1,0:T(8,128)}, f32[96,3072...) custom-call(s32[1,2]{1,0:T(1,128)} %refs_0_.1, s32[1,2,2]{2,1,0:T(2,128)} %refs_1_.1, ...), custom_call_target="tpu_custom_call" | custom-call | tf_op jit(solution)/shard_map/pallas_call | solution.py:1040
  247.4 4.7 %shard_map.145 = (bf16[2,256,768]{2,1,0:T(8,128)(2,1)}, bf16[2,256,768]{2,1,0:T(8,128)(2,1)}, f32[96,2304]{1,0:T(8,128)}, f32[96,768]{1,0:T(8,128)}, f32[96,3072...) custom-call(bf16[4,256,768]{2,1,0:T(8,128)(2,1)} %get-tuple-element.21.refs_0_, ...), custom_call_target="tpu_custom_call" | custom-call | tf_op jit(solution)/shard_map/pallas_call | solution.py:1139
